TPU v7x, 256 devices: a whole 4x4x8 slice. The times are simulated.
256 devices in a mesh: context: 32 (over z, y_hi, core), tensor: 8 (over y_lo, x).
Axes of the slice: x: 4, y: 4 (y_hi: 2, y_lo: 2; y = y_hi * 2 + y_lo), z: 8, core: 2. Of those that a mesh axis runs over, the one named last changes fastest.
Arguments:
- query_proj: bfloat16 [8192, 8192], P('context', 'tensor'), may hold values from -6 to 6
- key_proj: bfloat16 [8192, 8192], P('context', 'tensor'), may hold values from -6 to 6
- value_proj: bfloat16 [8192, 8192], P('context', 'tensor'), may hold values from -6 to 6
- short_taps: float32 [3, 3, 8192], P(None, None, 'tensor'), may hold values from -3 to 3
- long_filter: bfloat16 [8192, 8192], P('tensor', 'context'), may hold values from -0.0625 to 0.0625
- skip_weight: float32 [8192], P('tensor'), may hold values from -4 to 4
- out_weight: bfloat16 [8192, 4096], P('tensor'), may hold values from -0.09375 to 0.09375
- norm_gain: float32 [4096], P('tensor'), may hold values from 0.5 to 1.5
Outputs:
- normed: bfloat16 [8192, 4096], P('context', 'tensor')
All inputs are finite; a program needn't handle non-finite values.
Results may differ from a plain program's by a relative error of at most 0.019.
Values may be sent and summed in bfloat16 or wider, within the bound.
A program may use at most 64 MiB of HBM per device.

v0:
```python
import math

import jax
import jax.numpy as jnp
from jax import lax
from jax.sharding import PartitionSpec as P

E = 4096


highest = lax.Precision.HIGHEST


def passed_along(x, axis, by):
    size = lax.axis_size(axis)
    pairs = [(i, i + by) for i in range(size) if 0 <= i + by < size]
    return lax.ppermute(x, axis, pairs)


def featurize(values, before, taps):
    count = values.shape[0]
    extended = jnp.concatenate([before, values], axis=0).astype(jnp.float32)
    return taps[0] * extended[2:] + taps[1] * extended[1 : count + 1] + taps[2] * extended[:count]


def angle_table(rows, cols, period):
    product = lax.broadcasted_iota(jnp.int32, (rows, cols), 0) * lax.broadcasted_iota(
        jnp.int32, (rows, cols), 1
    )
    turns = (product % period).astype(jnp.float32) * (2.0 * math.pi / period)
    return (jnp.cos(turns), -jnp.sin(turns))


def forward_spectrum(samples, tables):
    outer_re, outer_im, twist_re, twist_im, inner_re, inner_im = tables
    half_factor = samples.shape[1]
    upper_re = jnp.einsum("ka,cab->ckb", outer_re[:, :half_factor], samples, precision=highest)
    upper_im = jnp.einsum("ka,cab->ckb", outer_im[:, :half_factor], samples, precision=highest)
    turned_re = upper_re * twist_re - upper_im * twist_im
    turned_im = upper_re * twist_im + upper_im * twist_re
    spec_re = jnp.einsum("ckb,bm->ckm", turned_re, inner_re, precision=highest) - jnp.einsum(
        "ckb,bm->ckm", turned_im, inner_im, precision=highest
    )
    spec_im = jnp.einsum("ckb,bm->ckm", turned_re, inner_im, precision=highest) + jnp.einsum(
        "ckb,bm->ckm", turned_im, inner_re, precision=highest
    )
    return (spec_re, spec_im)


def long_convolve(signal, kernel):
    channels, length = signal.shape
    padded_length = 2 * length
    first_factor = 128
    second_factor = padded_length // first_factor
    half_factor = first_factor // 2
    outer_re, outer_im = angle_table(first_factor, first_factor, first_factor)
    twist_re, twist_im = angle_table(first_factor, second_factor, padded_length)
    inner_re, inner_im = angle_table(second_factor, second_factor, second_factor)
    tables = (outer_re, outer_im, twist_re, twist_im, inner_re, inner_im)
    signal_re, signal_im = forward_spectrum(
        signal.astype(jnp.float32).reshape(channels, half_factor, second_factor), tables
    )
    kernel_re, kernel_im = forward_spectrum(
        kernel.astype(jnp.float32).reshape(channels, half_factor, second_factor), tables
    )
    prod_re = signal_re * kernel_re - signal_im * kernel_im
    prod_im = signal_re * kernel_im + signal_im * kernel_re
    back_re = jnp.einsum("ckm,mb->ckb", prod_re, inner_re, precision=highest) + jnp.einsum(
        "ckm,mb->ckb", prod_im, inner_im, precision=highest
    )
    back_im = jnp.einsum("ckm,mb->ckb", prod_im, inner_re, precision=highest) - jnp.einsum(
        "ckm,mb->ckb", prod_re, inner_im, precision=highest
    )
    untwist_re = back_re * twist_re + back_im * twist_im
    untwist_im = back_im * twist_re - back_re * twist_im
    result = jnp.einsum(
        "ak,ckb->cab", outer_re[:half_factor], untwist_re, precision=highest
    ) + jnp.einsum("ak,ckb->cab", outer_im[:half_factor], untwist_im, precision=highest)
    return (result * (1.0 / padded_length)).reshape(channels, length)


def per_device(
    query_proj, key_proj, value_proj, short_taps, long_filter, skip_weight, out_weight, norm_gain
):
    tokens_here = query_proj.shape[0]
    cut_at = tokens_here - 2
    before_query, before_key, before_value = passed_along(
        (query_proj[cut_at:], key_proj[cut_at:], value_proj[cut_at:]), "context", 1
    )
    query_feat = featurize(query_proj, before_query, short_taps[0])
    key_feat = featurize(key_proj, before_key, short_taps[1])
    value_feat = featurize(value_proj, before_value, short_taps[2])
    mixed_in = (key_feat * value_feat).astype(jnp.bfloat16)
    groups = lax.axis_size("context")
    local_width = mixed_in.shape[1]
    per_group = local_width // groups
    mixed_rows = mixed_in.T.reshape(groups, per_group, tokens_here)
    filter_rows = long_filter.reshape(groups, per_group, tokens_here)
    signal_piece = lax.all_to_all(mixed_rows, "context", split_axis=0, concat_axis=2, tiled=True)
    kernel_piece = lax.all_to_all(filter_rows, "context", split_axis=0, concat_axis=2, tiled=True)
    convolved_piece = long_convolve(signal_piece[0], kernel_piece[0]).astype(jnp.bfloat16)
    convolved = lax.all_to_all(
        convolved_piece[None], "context", split_axis=2, concat_axis=0, tiled=True
    )
    convolved = convolved.reshape(local_width, tokens_here).T
    gated = (
        query_feat * (convolved.astype(jnp.float32) + skip_weight * mixed_in.astype(jnp.float32))
    ).astype(jnp.bfloat16)
    partial_sum = jnp.dot(gated, out_weight, preferred_element_type=jnp.float32)
    total = lax.psum(partial_sum.astype(jnp.bfloat16), "tensor").astype(jnp.float32)
    meansq = jnp.sum(total * total, axis=1, keepdims=True) * (1.0 / E)
    share = norm_gain.shape[0]
    mine = lax.dynamic_slice_in_dim(total, lax.axis_index("tensor") * share, share, 1)
    return (mine * lax.rsqrt(meansq + 1e-06) * norm_gain).astype(jnp.bfloat16)


def solution(mesh):
    placed = (
        P("context", "tensor"),
        P("context", "tensor"),
        P("context", "tensor"),
        P(None, None, "tensor"),
        P("tensor", "context"),
        P("tensor"),
        P("tensor", None),
        P("tensor"),
    )
    return jax.shard_map(
        per_device, mesh=mesh, in_specs=placed, out_specs=P("context", "tensor"), check_vma=False
    )
```

profile of v0, /device:TPU:8, one launch (start us, length us, event | category | flops | bytes accessed | tf_op | source)
XLA Modules:
  0.0 301.9 jit_solution(611443979122815283)
XLA Ops:
  6.5 10.7 %all-to-all-start.1 = ((bf16[32,32,256]{2,1,0:T(8,128)(2,1)}), bf16[32,32,256]{2,1,0:T(8,128)(2,1)S(1)}, u32[]{:S(2)}, u32[]{:S(2)}) async-start(bf16[32,32,256]{2,1,0:T(8,128)(2,1)} %bitcast.150), calls=%async_computation.1 | async-start | bytes 1048576 | tf_op jit(solution)/shard_map/all_to_all | solution.py:100
  17.3 0.7 slice.110
  18.0 0.9 copy.146
  18.9 2.2 collective-permute-start.1
  21.1 0.7 slice.117
  21.8 0.9 copy.148
  22.7 5.0 %collective-permute-start.2 = (bf16[2,1024]{0,1:T(8,128)(2,1)}, bf16[2,1024]{0,1:T(8,128)(2,1)S(1)}, u32[]{:S(2)}, u32[]{:S(2)}) collective-permute-start(bf16[2,1024]{0,1:T(8,128)(2,1)} %copy.148), channel_id=1, source_target_pairs={{0,8},{8,16},{16,24},{24,32},{32,40},{40,48},{48,56},{56,64},{64,7... | collective-permute-start | bytes 12296 | tf_op jit(solution)/shard_map/ppermute | solution.py:17
  27.7 0.3 sine_negate_fusion
  28.0 0.3 fusion.82
  28.2 0.9 fusion.141
  29.2 0.3 sine_negate_fusion.1
  29.4 0.2 copy.147
  29.7 0.2 copy.149
  30.1 0.3 maximum_convert_fusion.2
  30.4 0.3 maximum_convert_fusion.1
  30.8 2.9 fusion.38
  33.6 1.7 all-to-all-done.1
  35.3 14.0 %all-to-all-start = ((bf16[32,32,256]{2,1,0:T(8,128)(2,1)}), bf16[32,32,256]{2,1,0:T(8,128)(2,1)S(1)}, u32[]{:S(2)}, u32[]{:S(2)}) async-start(bf16[32,32,256]{2,1,0:T(8,128)(2,1)} %bitcast.10), calls=%async_computation | async-start | bytes 1048576 | tf_op jit(solution)/shard_map/all_to_all | solution.py:99
  49.3 0.3 copy.155
  49.6 0.2 reshape.92
  49.8 1.0 fusion.91
  50.8 1.0 fusion.89
  51.8 2.2 fusion
  54.0 2.2 fusion.2
  56.2 2.2 fusion.21
  58.4 3.6 %fusion.18 = f32[32,128,128]{2,1,0:T(8,128)} fusion(f32[32,128,128]{2,1,0:T(8,128)S(1)} %fusion.2, f32[128,32,128]{2,0,1:T(8,128)S(1)} %fusion.91, f32[128,32,128]{2,0,1:T(8,128)S(1)} %fusion.89, f32[128,128]{1,0:T(8,128)S(1)} %copy.157, f32[128,128]{1,0:T(8,128)S(1)} %copy.156), kind=kOutput, calls=%fused_computation.28 | convolution fusion | flops 807632896 | bytes 8519680 | tf_op jit(solution)/shard_map/ckb,bm->ckm/dot_general | solution.py:41
  62.0 5.1 %all-to-all-done = bf16[32,32,256]{2,1,0:T(8,128)(2,1)S(1)} async-done(((bf16[32,32,256]{2,1,0:T(8,128)(2,1)}), bf16[32,32,256]{2,1,0:T(8,128)(2,1)S(1)}, u32[]{:S(2)}, u32[]{:S(2)}) %all-to-all-start) | async-done | bytes 524320 | tf_op jit(solution)/shard_map/all_to_all | solution.py:99
  67.2 0.3 copy.150
  67.5 0.2 reshape.90
  67.6 1.5 fusion.92
  69.1 1.2 fusion.90
  70.3 3.8 %fusion.52 = f32[32,128,128]{2,1,0:T(8,128)S(1)} fusion(f32[32,128,128]{2,1,0:T(8,128)S(1)} %fusion.92, f32[32,128,128]{2,1,0:T(8,128)S(1)} %fusion.90, f32[128,128]{0,1:T(8,128)S(1)} %get-tuple-element.16, f32[128,128]{0,1:T(8,128)S(1)} %get-tuple-element.17), kind=kOutput, calls=%fused_computation.66 | convolution fusion | flops 807124992 | bytes 6422528 | tf_op jit(solution)/shard_map/ckb,bm->ckm/dot_general | solution.py:44
  74.2 3.9 %fusion.54 = f32[32,128,128]{2,1,0:T(8,128)S(1)} fusion(f32[32,128,128]{2,1,0:T(8,128)S(1)} %fusion.92, f32[32,128,128]{2,1,0:T(8,128)S(1)} %fusion.90, f32[128,128]{0,1:T(8,128)S(1)} %get-tuple-element.16, f32[128,128]{0,1:T(8,128)S(1)} %get-tuple-element.17), kind=kOutput, calls=%fused_computation.67 | convolution fusion | flops 807108608 | bytes 6422528 | tf_op jit(solution)/shard_map/ckb,bm->ckm/dot_general | solution.py:41
  78.1 4.3 %convolution_subtract_fusion.1 = f32[32,128,128]{2,1,0:T(8,128)S(1)} fusion(f32[32,128,128]{2,1,0:T(8,128)S(1)} %fusion.54, f32[32,128,128]{2,1,0:T(8,128)S(1)} %fusion.92, f32[32,128,128]{2,1,0:T(8,128)S(1)} %fusion.90, f32[128,128]{0,1:T(8,128)S(1)} %get-tuple-element.16, f32[128,128]{0,1:T(8,128)S(1)} %get-tuple-element.17), kind=kOutput, calls=%fused_computation.33 | convolution fusion | flops 807649280 | bytes 8519680 | tf_op jit(solution)/shard_map/ckb,bm->ckm/dot_general | solution.py:41
  82.3 4.1 %multiply_add_fusion = (f32[32,128,128]{2,1,0:T(8,128)S(1)}, f32[32,128,128]{2,1,0:T(8,128)S(1)}) fusion(f32[32,128,128]{2,1,0:T(8,128)S(1)} %copy-done.1, f32[32,128,128]{2,1,0:T(8,128)S(1)} %convolution_subtract_fusion.1, f32[32,128,128]{2,1,0:T(8,128)S(1)} %fusion.21, f32[32,128,128]{2,1,0:T(8,128)S(1)} %fusion.52, f32[32,128,128]{2,1,0:T(8,128)S(1)} %fusion.92, ...), kind=kOutput, calls=%fused_computation.24 | convolution fusion | flops 810778624 | bytes 16908288 | tf_op jit(solution)/shard_map/ckb,bm->ckm/dot_general | solution.py:44
  86.5 2.2 fusion.66
  88.7 2.2 fusion.68
  91.0 2.3 convolution_subtract_fusion
  93.2 2.4 convolution_add_fusion
  95.7 2.6 fusion.10
  98.3 2.6 fusion.33
  100.9 0.2 convert_element_type.138
  101.2 6.7 %copy.178 = bf16[1,32,8192]{1,0,2:T(2,128)(2,1)} copy(bf16[1,32,8192]{2,1,0:T(8,128)(2,1)S(1)} %convert_element_type.138) | data formatting | bytes 1048576 | tf_op jit(solution)/shard_map/convert_element_type | solution.py:101
  107.8 0.5 broadcast.164
  108.3 45.4 %reduce = bf16[8192,32]{1,0:T(8,128)(2,1)S(1)} reduce(bf16[8192,1,32]{2,1,0:T(2,128)(2,1)} %bitcast.144, bf16[]{:T(256)} %broadcast.164), dimensions={1}, to_apply=%bitcast.125.reduce_sub_computation | reduce | bytes 1048578
  153.8 2.7 reshape.111
  156.5 4.7 %all-to-all-start.2 = ((bf16[32,2,4096]{2,1,0:T(2,128)(2,1)}), bf16[32,2,4096]{2,1,0:T(2,128)(2,1)S(1)}, u32[]{:S(2)}, u32[]{:S(2)}) async-start(bf16[32,2,4096]{2,1,0:T(2,128)(2,1)} %reshape.111), calls=%async_computation.2 | async-start | bytes 1048576 | tf_op jit(solution)/shard_map/all_to_all | solution.py:102
  161.2 0.2 copy.144
  161.4 2.2 collective-permute-start
  163.6 0.2 copy.145
  163.8 0.9 collective-permute-done
  164.8 0.3 maximum_convert_fusion
  165.1 14.1 %all-to-all-done.2 = bf16[32,2,4096]{2,1,0:T(2,128)(2,1)S(1)} async-done(((bf16[32,2,4096]{2,1,0:T(2,128)(2,1)}), bf16[32,2,4096]{2,1,0:T(2,128)(2,1)S(1)}, u32[]{:S(2)}, u32[]{:S(2)}) %all-to-all-start.2) | async-done | bytes 524320 | tf_op jit(solution)/shard_map/all_to_all | solution.py:102
  179.2 7.1 %reshape.112 = bf16[8192,1,32]{2,1,0:T(2,128)(2,1)} reshape(bf16[32,2,4096]{2,1,0:T(2,128)(2,1)S(1)} %all-to-all-done.2) | data formatting | bytes 1048576
  186.3 8.0 %copy.179 = bf16[1,32,8192]{2,1,0:T(8,128)(2,1)S(1)} copy(bf16[1,32,8192]{1,0,2:T(2,128)(2,1)} %bitcast.145) | data formatting | bytes 1048576 | tf_op jit(solution)/shard_map/all_to_all | solution.py:102
  194.2 0.1 copy.219
  194.5 0.6 copy.180
  195.1 2.3 fusion.44
  197.4 7.1 %convolution_convert_fusion = bf16[256,4096]{1,0:T(8,128)(2,1)} fusion(bf16[256,1024]{0,1:T(8,128)(2,1)S(1)} %fusion.44, bf16[1024,4096]{1,0:T(8,128)(2,1)} %param.14), kind=kOutput, calls=%fused_computation | convolution fusion | flops 2148532224 | bytes 11010048 | tf_op jit(solution)/shard_map/dot_general | solution.py:109
  204.5 86.6 %all-reduce.2.cloned.1.call-done = bf16[256,4096]{1,0:T(8,128)(2,1)} async-done(((bf16[256,4096]{1,0:T(8,128)(2,1)}), bf16[256,4096]{1,0:T(8,128)(2,1)}) %all-reduce.2.cloned.1.call-update) | async-done | bytes 2097168 | tf_op jit(solution)/shard_map/psum | solution.py:110
  291.1 2.2 multiply_reduce_fusion
  293.4 0.5 convert_element_type.147
  293.9 0.2 copy-done.6
  294.0 0.8 multiply_convert_fusion
  (22 shorter events, 0.4 us)
Async XLA Ops:
  6.5 22.9 %copy-start.2 = (bf16[256,1024]{1,0:T(8,128)(2,1)S(1)}, bf16[256,1024]{1,0:T(8,128)(2,1)}, u32[]{:S(2)}) copy-start(bf16[256,1024]{1,0:T(8,128)(2,1)} %param.9) | copy-start | bytes 1572868
  6.5 23.1 %copy-start.3 = (bf16[256,1024]{1,0:T(8,128)(2,1)S(1)}, bf16[256,1024]{1,0:T(8,128)(2,1)}, u32[]{:S(2)}) copy-start(bf16[256,1024]{1,0:T(8,128)(2,1)} %param.10) | copy-start | bytes 1572868
  6.5 28.8 %all-to-all-start.1 = ((bf16[32,32,256]{2,1,0:T(8,128)(2,1)}), bf16[32,32,256]{2,1,0:T(8,128)(2,1)S(1)}, u32[]{:S(2)}, u32[]{:S(2)}) async-start(bf16[32,32,256]{2,1,0:T(8,128)(2,1)} %bitcast.150), calls=%async_computation.1 | async-start | bytes 1048576 | tf_op jit(solution)/shard_map/all_to_all | solution.py:100
  18.9 11.6 %collective-permute-start.1 = (bf16[2,1024]{0,1:T(8,128)(2,1)}, bf16[2,1024]{0,1:T(8,128)(2,1)S(1)}, u32[]{:S(2)}, u32[]{:S(2)}) collective-permute-start(bf16[2,1024]{0,1:T(8,128)(2,1)} %copy.146), channel_id=1, source_target_pairs={{0,8},{8,16},{16,24},{24,32},{32,40},{40,48},{48,56},{56,64},{64,7... | collective-permute-start | bytes 12296 | tf_op jit(solution)/shard_map/ppermute | solution.py:17
  22.7 7.4 %collective-permute-start.2 = (bf16[2,1024]{0,1:T(8,128)(2,1)}, bf16[2,1024]{0,1:T(8,128)(2,1)S(1)}, u32[]{:S(2)}, u32[]{:S(2)}) collective-permute-start(bf16[2,1024]{0,1:T(8,128)(2,1)} %copy.148), channel_id=1, source_target_pairs={{0,8},{8,16},{16,24},{24,32},{32,40},{40,48},{48,56},{56,64},{64,7... | collective-permute-start | bytes 12296 | tf_op jit(solution)/shard_map/ppermute | solution.py:17
  35.3 31.9 %all-to-all-start = ((bf16[32,32,256]{2,1,0:T(8,128)(2,1)}), bf16[32,32,256]{2,1,0:T(8,128)(2,1)S(1)}, u32[]{:S(2)}, u32[]{:S(2)}) async-start(bf16[32,32,256]{2,1,0:T(8,128)(2,1)} %bitcast.10), calls=%async_computation | async-start | bytes 1048576 | tf_op jit(solution)/shard_map/all_to_all | solution.py:99
  78.0 4.3 %copy-start.1 = (f32[32,128,128]{2,1,0:T(8,128)S(1)}, f32[32,128,128]{2,1,0:T(8,128)}, u32[]{:S(2)}) copy-start(f32[32,128,128]{2,1,0:T(8,128)} %fusion.18) | copy-start | bytes 6291460
  153.8 7.4 %copy-start.4 = (bf16[256,1024]{1,0:T(8,128)(2,1)S(1)}, bf16[256,1024]{1,0:T(8,128)(2,1)}, u32[]{:S(2)}) copy-start(bf16[256,1024]{1,0:T(8,128)(2,1)} %param.8) | copy-start | bytes 1572868
  156.5 22.7 %all-to-all-start.2 = ((bf16[32,2,4096]{2,1,0:T(2,128)(2,1)}), bf16[32,2,4096]{2,1,0:T(2,128)(2,1)S(1)}, u32[]{:S(2)}, u32[]{:S(2)}) async-start(bf16[32,2,4096]{2,1,0:T(2,128)(2,1)} %reshape.111), calls=%async_computation.2 | async-start | bytes 1048576 | tf_op jit(solution)/shard_map/all_to_all | solution.py:102
  161.1 130.0 %all-reduce.2.cloned.1.call-start = ((), (), s32[]{:S(2)}) async-start(), calls=%async_computation.3 | async-start | bytes 4194304 | tf_op jit(solution)/shard_map/psum | solution.py:110
  161.4 3.3 %collective-permute-start = (bf16[2,1024]{0,1:T(8,128)(2,1)S(1)}, bf16[2,1024]{0,1:T(8,128)(2,1)S(1)}, u32[]{:S(2)}, u32[]{:S(2)}) collective-permute-start(bf16[2,1024]{0,1:T(8,128)(2,1)S(1)} %copy.144), channel_id=1, source_target_pairs={{0,8},{8,16},{16,24},{24,32},{32,40},{40,48},{48,56},{56,64},{64,7... | collective-permute-start | bytes 12296 | tf_op jit(solution)/shard_map/ppermute | solution.py:17
  194.4 0.7 copy-start.5
  291.1 2.2 copy-start
  293.3 0.7 copy-start.6
Sparse Core Ops, SparseCore 0:
  204.6 86.4 all-reduce.1
where the time goes:
time: 307 us; the launch traced here: 302 us
  waiting for transfers between devices  108 us (35%)
  other arithmetic  55.9 us (18%)
  matrix products  52.5 us (17%)
  starting transfers between devices  38.8 us (13%)
  local copies, waits for them, and re-layouts  32.3 us (11%)
  between operations  14 us (5%)
    psum x1, waiting for transfers between devices, per_device(): lax.psum(partial_sum.astype(jnp.bfloat16), 'tensor').astype(jnp.float32)  86.6 us
    unnamed x1, other arithmetic  45.4 us
    all_to_all x1, waiting for transfers between devices, per_device(): lax.all_to_all(convolved_piece[None], 'context', split_axis=2, concat_axi...  14.1 us
    all_to_all x1, starting transfers between devices, per_device(): lax.all_to_all(mixed_rows, 'context', split_axis=0, concat_axis=2, tiled=...  14 us
    unnamed x21, local copies, waits for them, and re-layouts  11.3 us
    all_to_all x1, starting transfers between devices, per_device(): lax.all_to_all(filter_rows, 'context', split_axis=0, concat_axis=2, tiled...  10.7 us
    ppermute x3, starting transfers between devices, passed_along(): return lax.ppermute(x, axis, pairs)  9.41 us
    all_to_all x1, local copies, waits for them, and re-layouts, per_device(): lax.all_to_all(convolved_piece[None], 'context', split_axis=2, concat_axi...  7.97 us
  transfers between devices with their start and end apart: 7, of which 5 were waited for; matrix products, arithmetic and copies ran while one was open for 7% of the time, Pallas kernels for 0%

commit v1 on v0

v1 whole, which is shorter than its diff:
```python
import functools
import math

import jax
import jax.numpy as jnp
import ml_dtypes
import numpy as np
from jax import lax
from jax.experimental import pallas as pl
from jax.experimental.pallas import tpu as pltpu
from jax.sharding import PartitionSpec as P

F32, BF16 = jnp.float32, jnp.bfloat16
CTX, TEN = "context", "tensor"
HALO = 16
LANES = 128
PART = 16
SHIFT = 0.25
INNER = 8
TOKENS_PER_PART = 128


def times(z, c):
    re, im = z
    cr, ci = float(c.real), float(c.imag)
    cr = 0.0 if abs(cr) < 1e-12 else cr
    ci = 0.0 if abs(ci) < 1e-12 else ci
    if im is None:
        if ci == 0.0:
            return (re if cr == 1.0 else re * cr, None)
        return (re * cr, re * ci)
    if ci == 0.0:
        return z if cr == 1.0 else (re * cr, im * cr)
    if cr == 0.0:
        return (im * -ci, re * ci)
    if abs(abs(cr) - abs(ci)) < 1e-12:
        plus, minus = re + im, re - im
        if (cr > 0) == (ci > 0):
            return (minus * cr, plus * cr)
        return (plus * cr, minus * ci)
    return (re * cr - im * ci, re * ci + im * cr)


def real_part_times(z, c):
    re, im = z
    cr, ci = float(c.real), float(c.imag)
    if im is None or abs(ci) < 1e-12:
        return re if cr == 1.0 else re * cr
    return re * cr - im * ci


def plus_minus(a, b):
    (ar, ai), (br, bi) = a, b
    if ai is None and bi is None:
        return (ar + br, None), (ar - br, None)
    if ai is None:
        return (ar + br, bi), (ar - br, -bi)
    if bi is None:
        return (ar + br, ai), (ar - br, ai)
    return (ar + br, ai + bi), (ar - br, ai - bi)


def dft(x, sign):
    n = len(x)
    if n == 1:
        return list(x)
    even, odd = dft(x[0::2], sign), dft(x[1::2], sign)
    low, high = [], []
    for k in range(n // 2):
        e, o = even[k], odd[k]
        if 4 * k == n and e[1] is not None and o[1] is not None:
            s = float(sign)
            one = (e[0] - o[1], e[1] + o[0])
            two = (e[0] + o[1], e[1] - o[0])
            a, b = (one, two) if s > 0 else (two, one)
        else:
            a, b = plus_minus(e, times(o, turn(sign * k / n)))
        low.append(a)
        high.append(b)
    return low + high


def turn(x):
    return complex(math.cos(2 * math.pi * x), math.sin(2 * math.pi * x))


def im_of(z):
    return jnp.zeros_like(z[0]) if z[1] is None else z[1]


def split_table(x):
    high = x.astype(ml_dtypes.bfloat16)
    low = (x - high.astype(np.float64)).astype(ml_dtypes.bfloat16)
    return np.stack([high, low])


def tables(blocks):
    length = blocks * LANES
    t = np.arange(LANES)
    phase = np.outer(t, t) % LANES / LANES
    forward = np.exp(-2j * np.pi * phase)
    backward = np.exp(2j * np.pi * phase) / length
    pair = lambda w: np.block([[w.real, w.imag], [-w.imag, w.real]])
    twist = np.exp(-2j * np.pi * np.outer(np.arange(blocks) + SHIFT, t) / length)
    return (
        split_table(pair(forward)),
        split_table(pair(backward)),
        np.stack([twist.real, twist.imag]).astype(np.float32),
    )


def kernel(
    nc,
    nt,
    q_hbm,
    k_hbm,
    v_hbm,
    filt_hbm,
    w_hbm,
    fwd_hbm,
    bwd_hbm,
    taps,
    skip,
    gain,
    twist,
    out,
    qbuf,
    kbuf,
    vbuf,
    wbuf,
    fwd,
    bwd,
    qfeat,
    mixed,
    mixed_t,
    frecv,
    srecv,
    csend,
    crecv,
    mid,
    high,
    low,
    fspec,
    dspec,
    gated,
    psend,
    precv,
    total,
    ssend,
    srow,
    load_sem,
    halo_send,
    halo_recv,
    filt_send,
    filt_recv,
    sig_send,
    sig_recv,
    conv_send,
    conv_recv,
    part_send,
    part_recv,
    row_send,
    row_recv,
):
    me, mt = lax.axis_index(CTX), lax.axis_index(TEN)
    tokens, width = q_hbm.shape
    per = width // nc
    parts = per // PART
    halves = tokens // LANES
    blocks = nc * halves
    outer = blocks // INNER
    step_s = INNER // halves
    share = out.shape[1]
    chunks = tokens // TOKENS_PER_PART

    def partner(j, mine, n):
        step = j // 2 + 1
        odd = j % 2
        return (mine + step * (1 - odd) + (n - step) * odd) % n

    def remote(src, dst, send, recv, device):
        return pltpu.make_async_remote_copy(
            src_ref=src,
            dst_ref=dst,
            send_sem=send,
            recv_sem=recv,
            device_id=device,
            device_id_type=pl.DeviceIdType.MESH,
        )

    body = pl.ds(HALO, tokens)
    loads = [
        pltpu.make_async_copy(src, dst, load_sem.at[i])
        for i, (src, dst) in enumerate(
            (
                (k_hbm, kbuf.at[body, :]),
                (v_hbm, vbuf.at[body, :]),
                (q_hbm, qbuf.at[body, :]),
                (fwd_hbm, fwd),
                (bwd_hbm, bwd),
                (w_hbm, wbuf),
            )
        )
    ]
    for copy in loads:
        copy.start()

    barrier = pltpu.get_barrier_semaphore()

    @pl.loop(0, nc - 1)
    def _(j):
        pl.semaphore_signal(barrier, inc=1, device_id={CTX: partner(j, me, nc)})

    @pl.loop(0, nt - 1)
    def _(j):
        pl.semaphore_signal(barrier, inc=1, device_id={TEN: partner(j, mt, nt)})

    pl.semaphore_wait(barrier, nc - 1 + nt - 1)

    halos = [
        remote(
            src.at[pl.ds(tokens - HALO, HALO), :],
            dst.at[pl.ds(0, HALO), :],
            halo_send.at[i],
            halo_recv.at[i],
            {CTX: (me + 1) % nc},
        )
        for i, (src, dst) in enumerate(((k_hbm, kbuf), (v_hbm, vbuf), (q_hbm, qbuf)))
    ]

    @pl.when(me < nc - 1)
    def _():
        for copy in halos:
            copy.start()

    @pl.when(me == 0)
    def _():
        for buf in (kbuf, vbuf, qbuf):
            buf[pl.ds(0, HALO), :] = jnp.zeros((HALO, width), BF16)

    def filter_copy(p):
        return remote(
            filt_hbm.at[pl.ds(pl.multiple_of(p * per, PART), per), :],
            frecv.at[me],
            filt_send.at[p],
            filt_recv.at[me],
            {CTX: p},
        )

    @pl.loop(0, nc - 1)
    def _(j):
        filter_copy(partner(j, me, nc)).start()

    own_filter = pltpu.make_async_copy(
        filt_hbm.at[pl.ds(pl.multiple_of(me * per, PART), per), :], frecv.at[me], filt_recv.at[me]
    )
    own_filter.start()

    def feature(buf, r, row, lane):
        wide = buf[pl.ds(row, LANES + HALO), lane].astype(F32)[HALO - 8 :]
        one = pltpu.roll(wide, 1, 0)[8:]
        two = pltpu.roll(wide, 2, 0)[8:]
        return (
            taps[r, pl.ds(0, 1), lane] * wide[8:]
            + taps[r, pl.ds(1, 1), lane] * one
            + taps[r, pl.ds(2, 1), lane] * two
        )

    columns = width // LANES

    def place(i):
        row = pl.multiple_of(i // columns * LANES, LANES)
        col = pl.multiple_of(i % columns * LANES, LANES)
        return row, col

    for i in (0, 1):
        loads[i].wait()

    @pl.when(me > 0)
    def _():
        for i in (0, 1):
            halos[i].wait_recv()

    @pl.loop(0, halves * columns)
    def _(i):
        row, col = place(i)
        lane = pl.ds(col, LANES)
        product = feature(kbuf, 1, row, lane) * feature(vbuf, 2, row, lane)
        mixed[pl.ds(row, LANES), lane] = product.astype(BF16)
        mixed_t[pl.ds(col, LANES), pl.ds(row, LANES)] = product.T.astype(BF16)

    def signal_copy(part, p):
        return remote(
            mixed_t.at[pl.ds(pl.multiple_of(p * per + part * PART, PART), PART), :],
            srecv.at[me, pl.ds(part * PART, PART), :],
            sig_send.at[part, p],
            sig_recv.at[part, me],
            {CTX: p},
        )

    for part in range(parts):

        @pl.loop(0, nc - 1)
        def _(j):
            signal_copy(part, partner(j, me, nc)).start()

        pltpu.make_async_copy(
            mixed_t.at[pl.ds(pl.multiple_of(me * per + part * PART, PART), PART), :],
            srecv.at[me, pl.ds(part * PART, PART), :],
            sig_recv.at[part, me],
        ).start()

    loads[2].wait()

    @pl.when(me > 0)
    def _():
        halos[2].wait_recv()

    @pl.loop(0, halves * columns)
    def _(i):
        row, col = place(i)
        lane = pl.ds(col, LANES)
        qfeat[pl.ds(row, LANES), lane] = feature(qbuf, 0, row, lane)

    def block_of(k1):
        return pl.ds(k1 * PART, PART)

    left, right = pl.ds(0, LANES), pl.ds(LANES, LANES)

    def outer_forward(recv, part):
        rows = pl.ds(pl.multiple_of(part * PART, PART), PART)
        for b in range(INNER):
            lane = pl.ds(b % halves * LANES, LANES)
            x = [
                times((recv[step_s * a + b // halves, rows, lane].astype(F32), None), turn(-a * SHIFT / outer))
                for a in range(outer)
            ]
            for q, z in enumerate(dft(x, -1)):
                re, im = times(z, turn(-b * (q + SHIFT) / blocks))
                mid[b, q, 0] = re
                mid[b, q, 1] = jnp.zeros_like(re) if im is None else im
        for q in range(outer):
            y = [(mid[b, q, 0], mid[b, q, 1]) for b in range(INNER)]
            for r, (re, im) in enumerate(dft(y, -1)):
                k1 = q + outer * r
                cos, sin = twist[0, pl.ds(k1, 1), :], twist[1, pl.ds(k1, 1), :]
                put(k1 * PART, re * cos - im * sin, im * cos + re * sin)

    def put(row, re, im):
        rows = pl.ds(row, re.shape[0])
        for lane, x in ((left, re), (right, im)):
            top = x.astype(BF16)
            high[rows, lane] = top
            low[rows, lane] = (x - top.astype(F32)).astype(BF16)

    def product(rows, table):
        a, b = high[rows, :], low[rows, :]
        dot = functools.partial(jnp.dot, preferred_element_type=F32)
        return dot(a, table[0]) + dot(b, table[0]) + dot(a, table[1])

    tall = min(256, blocks * PART)

    @pl.loop(0, nc)
    def _(s):
        pltpu.make_async_copy(frecv.at[s], frecv.at[s], filt_recv.at[s]).wait()

    for i in (3, 4):
        loads[i].wait()

    @pl.loop(0, parts)
    def _(part):
        outer_forward(frecv, part)

        @pl.loop(0, blocks * PART // tall)
        def _(i):
            rows = pl.ds(pl.multiple_of(i * tall, tall), tall)
            fspec[part, rows, :] = product(rows, fwd)

    def conv_copy(part, p):
        return remote(
            csend.at[p, pl.ds(pl.multiple_of(part * PART, PART), PART), :],
            crecv.at[pl.ds(pl.multiple_of(me * per + part * PART, PART), PART), :],
            conv_send.at[part, p],
            conv_recv.at[part, me],
            {CTX: p},
        )

    @pl.loop(0, parts)
    def _(part):
        rows16 = pl.ds(pl.multiple_of(part * PART, PART), PART)

        @pl.loop(0, nc)
        def _(s):
            slot = srecv.at[s, rows16, :]
            pltpu.make_async_copy(slot, slot, sig_recv.at[part, s]).wait()

        outer_forward(srecv, part)

        @pl.loop(0, blocks * PART // tall)
        def _(i):
            start = pl.multiple_of(i * tall, tall)
            rows = pl.ds(start, tall)
            spec = product(rows, fwd)
            re, im = spec[:, :LANES], spec[:, LANES:]
            fre, fim = fspec[part, rows, left], fspec[part, rows, right]
            put(start, re * fre - im * fim, re * fim + im * fre)
            dspec[rows, :] = product(rows, bwd)

        for q in range(outer):
            y = []
            for r in range(INNER):
                k1 = q + outer * r
                cos, sin = twist[0, pl.ds(k1, 1), :], twist[1, pl.ds(k1, 1), :]
                re, im = dspec[block_of(k1), left], dspec[block_of(k1), right]
                y.append((re * cos + im * sin, im * cos - re * sin))
            for b, z in enumerate(dft(y, 1)):
                re, im = times(z, turn(b * (q + SHIFT) / blocks))
                mid[b, q, 0] = re
                mid[b, q, 1] = im
        for b in range(INNER):
            lane = pl.ds(b % halves * LANES, LANES)
            y = [(mid[b, q, 0], mid[b, q, 1]) for q in range(outer)]
            for a, z in enumerate(dft(y, 1)):
                csend[step_s * a + b // halves, rows16, lane] = real_part_times(
                    z, turn(a * SHIFT / outer)
                ).astype(BF16)

        @pl.loop(0, nc - 1)
        def _(j):
            conv_copy(part, partner(j, me, nc)).start()

        pltpu.make_async_copy(
            csend.at[me, rows16, :],
            crecv.at[pl.ds(pl.multiple_of(me * per + part * PART, PART), PART), :],
            conv_recv.at[part, me],
        ).start()

    for part in range(parts):

        @pl.loop(0, nc)
        def _(s):
            slot = crecv.at[pl.ds(pl.multiple_of(s * per + part * PART, PART), PART), :]
            pltpu.make_async_copy(slot, slot, conv_recv.at[part, s]).wait()

    @pl.loop(0, halves * columns)
    def _(i):
        row, col = place(i)
        lane, rows = pl.ds(col, LANES), pl.ds(row, LANES)
        conv = crecv[lane, rows].astype(F32).T
        gated[rows, lane] = (
            qfeat[rows, lane] * (conv + skip[:, lane] * mixed[rows, lane].astype(F32))
        ).astype(BF16)

    loads[5].wait()

    def rows_of(chunk):
        return pl.ds(chunk * TOKENS_PER_PART, TOKENS_PER_PART)

    def term(chunk, p):
        return jnp.dot(
            gated[rows_of(chunk), :],
            wbuf[:, pl.ds(pl.multiple_of(p * share, LANES), share)],
            preferred_element_type=F32,
        ).astype(BF16)

    def part_copy(chunk, p):
        return remote(
            psend.at[p, rows_of(chunk), :],
            precv.at[mt, rows_of(chunk), :],
            part_send.at[chunk, p],
            part_recv.at[chunk, mt],
            {TEN: p},
        )

    for chunk in range(chunks):

        @pl.loop(0, nt - 1)
        def _(j):
            p = partner(j, mt, nt)
            psend[p, rows_of(chunk), :] = term(chunk, p)
            part_copy(chunk, p).start()

        precv[mt, rows_of(chunk), :] = term(chunk, mt)

    def row_copy(chunk, p):
        return remote(
            ssend.at[chunk], srow.at[chunk, mt], row_send.at[chunk, p], row_recv.at[chunk, mt], {TEN: p}
        )

    for chunk in range(chunks):

        @pl.loop(0, nt - 1)
        def _(j):
            p = partner(j, mt, nt)
            slot = precv.at[p, rows_of(chunk), :]
            pltpu.make_async_copy(slot, slot, part_recv.at[chunk, p]).wait()

        here = rows_of(chunk)
        squares = jnp.zeros((TOKENS_PER_PART, LANES), F32)
        for c in range(share // LANES):
            lane = pl.ds(c * LANES, LANES)
            s = precv[0, here, lane].astype(F32)
            for g in range(1, nt):
                s = s + precv[g, here, lane].astype(F32)
            total[here, lane] = s
            squares = squares + s * s
        sums = jnp.sum(squares, axis=1, keepdims=True)
        ssend[chunk] = jnp.broadcast_to(sums, (TOKENS_PER_PART, LANES)).T[:8]
        srow[chunk, mt] = ssend[chunk]

        @pl.loop(0, nt - 1)
        def _(j):
            row_copy(chunk, partner(j, mt, nt)).start()

    for chunk in range(chunks):

        @pl.loop(0, nt - 1)
        def _(j):
            p = partner(j, mt, nt)
            slot = srow.at[chunk, p]
            pltpu.make_async_copy(slot, slot, row_recv.at[chunk, p]).wait()

        here = rows_of(chunk)
        s = srow[chunk, 0]
        for g in range(1, nt):
            s = s + srow[chunk, g]
        scale = lax.rsqrt(s * (1.0 / (share * nt)) + 1e-06)
        scale = jnp.broadcast_to(scale[:1], (LANES, TOKENS_PER_PART)).T
        for c in range(share // LANES):
            lane = pl.ds(c * LANES, LANES)
            out[here, lane] = (total[here, lane] * scale * gain[:, lane]).astype(BF16)

    @pl.when(me < nc - 1)
    def _():
        for copy in halos:
            copy.wait_send()

    @pl.loop(0, nc - 1)
    def _(j):
        p = partner(j, me, nc)
        filter_copy(p).wait_send()
        for part in range(parts):
            signal_copy(part, p).wait_send()
            conv_copy(part, p).wait_send()

    @pl.loop(0, nt - 1)
    def _(j):
        p = partner(j, mt, nt)
        for chunk in range(chunks):
            part_copy(chunk, p).wait_send()
            row_copy(chunk, p).wait_send()


def per_device(
    query_proj, key_proj, value_proj, short_taps, long_filter, skip_weight, out_weight, norm_gain
):
    nc, nt = lax.axis_size(CTX), lax.axis_size(TEN)
    tokens, width = query_proj.shape
    features = out_weight.shape[1]
    share = features // nt
    per = width // nc
    parts = per // PART
    blocks = nc * (tokens // LANES)
    outer = blocks // INNER
    chunks = tokens // TOKENS_PER_PART
    fwd, bwd, twist = (jnp.asarray(x) for x in tables(blocks))
    anywhere = pl.BlockSpec(memory_space=pl.ANY)
    vmem = pl.BlockSpec(memory_space=pltpu.VMEM)
    dma = pltpu.SemaphoreType.DMA
    return pl.pallas_call(
        functools.partial(kernel, nc, nt),
        out_shape=jax.ShapeDtypeStruct((tokens, share), BF16),
        in_specs=[anywhere] * 7 + [vmem] * 4,
        out_specs=vmem,
        scratch_shapes=[
            pltpu.VMEM((tokens + HALO, width), BF16),
            pltpu.VMEM((tokens + HALO, width), BF16),
            pltpu.VMEM((tokens + HALO, width), BF16),
            pltpu.VMEM((width, features), BF16),
            pltpu.VMEM(fwd.shape, BF16),
            pltpu.VMEM(bwd.shape, BF16),
            pltpu.VMEM((tokens, width), F32),
            pltpu.VMEM((tokens, width), BF16),
            pltpu.VMEM((width, tokens), BF16),
            pltpu.VMEM((nc, per, tokens), BF16),
            pltpu.VMEM((nc, per, tokens), BF16),
            pltpu.VMEM((nc, per, tokens), BF16),
            pltpu.VMEM((width, tokens), BF16),
            pltpu.VMEM((INNER, outer, 2, PART, LANES), F32),
            pltpu.VMEM((blocks * PART, 2 * LANES), BF16),
            pltpu.VMEM((blocks * PART, 2 * LANES), BF16),
            pltpu.VMEM((parts, blocks * PART, 2 * LANES), F32),
            pltpu.VMEM((blocks * PART, 2 * LANES), F32),
            pltpu.VMEM((tokens, width), BF16),
            pltpu.VMEM((nt, tokens, share), BF16),
            pltpu.VMEM((nt, tokens, share), BF16),
            pltpu.VMEM((tokens, share), F32),
            pltpu.VMEM((chunks, 8, TOKENS_PER_PART), F32),
            pltpu.VMEM((chunks, nt, 8, TOKENS_PER_PART), F32),
            dma((6,)),
            dma((3,)),
            dma((3,)),
            dma((nc,)),
            dma((nc,)),
            dma((parts, nc)),
            dma((parts, nc)),
            dma((parts, nc)),
            dma((parts, nc)),
            dma((chunks, nt)),
            dma((chunks, nt)),
            dma((chunks, nt)),
            dma((chunks, nt)),
        ],
        compiler_params=pltpu.CompilerParams(
            collective_id=0, has_side_effects=True, vmem_limit_bytes=56 * 1024 * 1024
        ),
    )(
        query_proj,
        key_proj,
        value_proj,
        long_filter,
        out_weight,
        fwd,
        bwd,
        short_taps,
        skip_weight.reshape(1, width),
        norm_gain.reshape(1, share),
        twist,
    )


def solution(mesh):
    placed = (
        P(CTX, TEN),
        P(CTX, TEN),
        P(CTX, TEN),
        P(None, None, TEN),
        P(TEN, CTX),
        P(TEN),
        P(TEN, None),
        P(TEN),
    )
    return jax.shard_map(
        per_device, mesh=mesh, in_specs=placed, out_specs=P(CTX, TEN), check_vma=False
    )
```

time: 307 us -> 96.4 us (0.31); the launches traced: 302 us -> 96.2 us
  waiting for transfers between devices: 108 us -> 0 us
  Pallas kernels: 0 us -> 94.5 us
  other arithmetic: 55.9 us -> 0 us
  matrix products: 52.5 us -> 0 us
  starting transfers between devices: 38.8 us -> 0 us
  local copies, waits for them, and re-layouts: 32.3 us -> 1.67 us
  between operations: 14 us -> 0.01 us
    pallas_call x0 -> x1, Pallas kernels: none -> 94.5 us  [per_device(): pl.pallas_call(functools.partial(kernel, nc, nt), out_shape=jax.ShapeDtyp...]
    psum x1 -> x0, waiting for transfers between devices: 86.6 us -> none  [per_device(): lax.psum(partial_sum.astype(jnp.bfloat16), 'tensor').astype(jnp.float32)]
    dot_general x19 -> x0, matrix products: 52.5 us -> none  [the longest x2 7.47 us: forward_spectrum(): jnp.einsum('ckb,bm->ckm', turned_re, inner_re, precision=highest)]
    unnamed x1 -> x0, other arithmetic: 45.4 us -> none
    all_to_all x3 -> x0, starting transfers between devices: 29.4 us -> none  [the longest x1 14 us: per_device(): lax.all_to_all(mixed_rows, 'context', split_axis=0, concat_axis=2, tiled=...]
    all_to_all x3 -> x0, waiting for transfers between devices: 20.8 us -> none  [the longest x1 14.1 us: per_device(): lax.all_to_all(convolved_piece[None], 'context', split_axis=2, concat_axi...]
    unnamed x21 -> x1, local copies, waits for them, and re-layouts: 11.3 us -> 1.67 us
    ppermute x3 -> x0, starting transfers between devices: 9.41 us -> none  [passed_along(): return lax.ppermute(x, axis, pairs)]
  transfers between devices with their start and end apart: 7 -> 0, of which waited for: 5 -> 0; matrix products, arithmetic and copies ran while one was open for 7% -> 0% of each run, Pallas kernels for 0% -> 0%
where the time goes in v1:
time: 96.4 us; the launch traced here: 96.2 us
  Pallas kernels  94.5 us (98%)
  local copies, waits for them, and re-layouts  1.67 us (2%)
    pallas_call x1, Pallas kernels, per_device(): pl.pallas_call(functools.partial(kernel, nc, nt), out_shape=jax.ShapeDtyp...  94.5 us

profile of v1, /device:TPU:8, one launch (start us, length us, event | category | flops | bytes accessed | tf_op | source)
XLA Modules:
  0.0 96.2 jit_solution(12517651018304057516)
XLA Ops:
  0.0 94.5 %shard_map.109 = bf16[256,512]{1,0:T(8,128)(2,1)} custom-call(bf16[256,1024]{1,0:T(8,128)(2,1)} %q_hbm.1, bf16[256,1024]{1,0:T(8,128)(2,1)} %k_hbm.1, bf16[256,1024]{1,0:T(8,128)(2,1)} %v_hbm.1, bf16[1024,256]{1,0:T(8,128)(2,1)} %filt_hbm.1, bf16[1024,4096]{1,0:T(8,128)(2,1)} %w_hbm.1, bf16[2,256,256]{2,1,0:T(8,128)(2,1)} %constant.6.clone.fwd_hbm, ...), custom_call_target="tpu_custom_call" | custom-call | tf_op jit(solution)/shard_map/pallas_call | solution.py:570
  94.5 1.7 %copy.13 = bf16[256,512]{1,0:T(8,128)(2,1)} copy(bf16[256,512]{1,0:T(8,128)(2,1)} %shard_map.109) | data formatting | bytes 524288

commit v2 on v1

--- a/solution.py
+++ b/solution.py
@@ -17,7 +17,8 @@
 PART = 16
 SHIFT = 0.25
 INNER = 8
-TOKENS_PER_PART = 128
+RING = 4
+PIECE = 64
 
 
 def times(z, c):
@@ -143,9 +144,16 @@
     fspec,
     dspec,
     gated,
-    psend,
-    precv,
-    total,
+    far,
+    relay,
+    to_right,
+    to_left,
+    from_left,
+    from_right,
+    own,
+    to_pair,
+    from_pair,
+    mine,
     ssend,
     srow,
     load_sem,
@@ -157,8 +165,8 @@
     sig_recv,
     conv_send,
     conv_recv,
-    part_send,
-    part_recv,
+    red_send,
+    red_recv,
     row_send,
     row_recv,
 ):
@@ -171,10 +179,9 @@
     outer = blocks // INNER
     step_s = INNER // halves
     share = out.shape[1]
-    chunks = tokens // TOKENS_PER_PART
 
     def partner(j, mine, n):
-        step = j // 2 + 1
+        step = n // 2 - (j + 1) // 2
         odd = j % 2
         return (mine + step * (1 - odd) + (n - step) * odd) % n
 
@@ -216,6 +223,34 @@
         pl.semaphore_signal(barrier, inc=1, device_id={TEN: partner(j, mt, nt)})
 
     pl.semaphore_wait(barrier, nc - 1 + nt - 1)
+
+    def settle(stage):
+        @pl.when(me < nc - 1)
+        def _():
+            for copy in halos:
+                copy.wait_send()
+
+        @pl.loop(0, nc - 1)
+        def _(j):
+            p = partner(j, me, nc)
+            filter_copy(p).wait_send()
+            if stage > 2:
+                for part in range(parts):
+                    signal_copy(part, p).wait_send()
+            if stage > 4:
+                for group in range(parts + halves - 1):
+                    conv_copy(group, p).wait_send()
+
+        if stage > 6:
+            for c in range(halves):
+                for u in pieces:
+                    for kind in range(7):
+                        message(kind, c, u).wait_send()
+
+            @pl.loop(0, nt - 1)
+            def _(j):
+                for c in range(halves):
+                    row_copy(c, partner(j, mt, nt)).wait_send()
 
     halos = [
         remote(
@@ -376,14 +411,33 @@
             rows = pl.ds(pl.multiple_of(i * tall, tall), tall)
             fspec[part, rows, :] = product(rows, fwd)
 
-    def conv_copy(part, p):
+    def conv_slice(group, p):
+        if isinstance(group, int) and group >= parts:
+            return pl.ds(pl.multiple_of(p * per, PART), per), pl.ds((group - parts + 1) * LANES, LANES)
+        return pl.ds(pl.multiple_of(p * per + group * PART, PART), PART), left
+
+    def conv_copy(group, p):
+        src = csend.at[p, conv_slice(group, 0)[0], conv_slice(group, 0)[1]]
         return remote(
-            csend.at[p, pl.ds(pl.multiple_of(part * PART, PART), PART), :],
-            crecv.at[pl.ds(pl.multiple_of(me * per + part * PART, PART), PART), :],
-            conv_send.at[part, p],
-            conv_recv.at[part, me],
-            {CTX: p},
+            src, crecv.at[conv_slice(group, me)], conv_send.at[group, p], conv_recv.at[group, me], {CTX: p}
         )
+
+    def send_conv(group):
+        @pl.loop(0, nc - 1)
+        def _(j):
+            conv_copy(group, partner(j, me, nc)).start()
+
+        pltpu.make_async_copy(
+            csend.at[me, conv_slice(group, 0)[0], conv_slice(group, 0)[1]],
+            crecv.at[conv_slice(group, me)],
+            conv_recv.at[group, me],
+        ).start()
+
+    def await_conv(group):
+        @pl.loop(0, nc)
+        def _(s):
+            slot = crecv.at[conv_slice(group, s)]
+            pltpu.make_async_copy(slot, slot, conv_recv.at[group, s]).wait()
 
     @pl.loop(0, parts)
     def _(part):
@@ -425,130 +479,160 @@
                     z, turn(a * SHIFT / outer)
                 ).astype(BF16)
 
-        @pl.loop(0, nc - 1)
-        def _(j):
-            conv_copy(part, partner(j, me, nc)).start()
-
-        pltpu.make_async_copy(
-            csend.at[me, rows16, :],
-            crecv.at[pl.ds(pl.multiple_of(me * per + part * PART, PART), PART), :],
-            conv_recv.at[part, me],
-        ).start()
-
-    for part in range(parts):
-
-        @pl.loop(0, nc)
-        def _(s):
-            slot = crecv.at[pl.ds(pl.multiple_of(s * per + part * PART, PART), PART), :]
-            pltpu.make_async_copy(slot, slot, conv_recv.at[part, s]).wait()
-
-    @pl.loop(0, halves * columns)
-    def _(i):
-        row, col = place(i)
-        lane, rows = pl.ds(col, LANES), pl.ds(row, LANES)
-        conv = crecv[lane, rows].astype(F32).T
-        gated[rows, lane] = (
-            qfeat[rows, lane] * (conv + skip[:, lane] * mixed[rows, lane].astype(F32))
-        ).astype(BF16)
-
-    loads[5].wait()
+        send_conv(part)
+
+    for half in range(1, halves):
+        send_conv(parts + half - 1)
+
+    def gate(chunk):
+        for group in range(parts) if chunk == 0 else [parts + chunk - 1]:
+            await_conv(group)
+        rows = rows_of(chunk)
+
+        @pl.loop(0, columns)
+        def _(i):
+            lane = pl.ds(pl.multiple_of(i * LANES, LANES), LANES)
+            conv = crecv[lane, rows].astype(F32).T
+            gated[rows, lane] = (
+                qfeat[rows, lane] * (conv + skip[:, lane] * mixed[rows, lane].astype(F32))
+            ).astype(BF16)
 
     def rows_of(chunk):
-        return pl.ds(chunk * TOKENS_PER_PART, TOKENS_PER_PART)
-
-    def term(chunk, p):
-        return jnp.dot(
-            gated[rows_of(chunk), :],
-            wbuf[:, pl.ds(pl.multiple_of(p * share, LANES), share)],
-            preferred_element_type=F32,
-        ).astype(BF16)
-
-    def part_copy(chunk, p):
-        return remote(
-            psend.at[p, rows_of(chunk), :],
-            precv.at[mt, rows_of(chunk), :],
-            part_send.at[chunk, p],
-            part_recv.at[chunk, mt],
-            {TEN: p},
-        )
-
-    for chunk in range(chunks):
-
-        @pl.loop(0, nt - 1)
-        def _(j):
-            p = partner(j, mt, nt)
-            psend[p, rows_of(chunk), :] = term(chunk, p)
-            part_copy(chunk, p).start()
-
-        precv[mt, rows_of(chunk), :] = term(chunk, mt)
+        return pl.ds(chunk * LANES, LANES)
+
+    ring_at, pair_at = mt % RING, mt // RING
+    rightward = {TEN: pair_at * RING + (ring_at + 1) % RING}
+    leftward = {TEN: pair_at * RING + (ring_at + RING - 1) % RING}
+    across = {TEN: (1 - pair_at) * RING + ring_at}
+
+    def term(chunk, pair, ring):
+        column = pl.multiple_of((pair * RING + ring) * share, LANES)
+        return jnp.dot(gated[rows_of(chunk), :], wbuf[:, pl.ds(column, share)], preferred_element_type=F32)
+
+    def terms(chunk, ring, into):
+        @pl.loop(0, 2)
+        def _(pair):
+            into[chunk, pair] = term(chunk, pair, ring % RING).astype(into.dtype)
+
+    def piece(u):
+        return pl.ds(u * PIECE, PIECE)
+
+    def first(u):
+        return pl.ds(u * PIECE, PIECE // 2)
+
+    def second(u):
+        return pl.ds(u * PIECE + PIECE // 2, PIECE // 2)
+
+    def message(kind, c, u):
+        src, dst, device = (
+            lambda: (far.at[c, :, first(u)], relay.at[c, :, first(u)], rightward),
+            lambda: (far.at[c, :, second(u)], relay.at[c, :, second(u)], leftward),
+            lambda: (to_right.at[c, :, second(u)], from_left.at[c, :, second(u)], rightward),
+            lambda: (to_left.at[c, :, first(u)], from_right.at[c, :, first(u)], leftward),
+            lambda: (to_right.at[c, :, first(u)], from_left.at[c, :, first(u)], rightward),
+            lambda: (to_left.at[c, :, second(u)], from_right.at[c, :, second(u)], leftward),
+            lambda: (to_pair.at[c, piece(u)], from_pair.at[c, piece(u)], across),
+        )[kind]()
+        return remote(src, dst, red_send.at[kind, c, u], red_recv.at[kind, c, u], device)
+
+    pieces = range(LANES // PIECE)
+
+    def start_ring(c):
+        terms(c, ring_at + 2, far)
+        for u in pieces:
+            message(0, c, u).start()
+            message(1, c, u).start()
+        terms(c, ring_at + 1, to_right)
+        for u in pieces:
+            message(2, c, u).start()
+        terms(c, ring_at + RING - 1, to_left)
+        for u in pieces:
+            message(3, c, u).start()
+        terms(c, ring_at, own)
+
+    def pass_on(c):
+        for u in pieces:
+            for kind, rows, buf in ((0, first(u), to_right), (1, second(u), to_left)):
+                message(kind, c, u).wait_recv()
+                for pair in range(2):
+                    buf[c, pair, rows] = (
+                        buf[c, pair, rows].astype(F32) + relay[c, pair, rows].astype(F32)
+                    ).astype(BF16)
+                message(kind + 4, c, u).start()
+
+    def end_ring(c):
+        for u in pieces:
+            for kind in (2, 3, 4, 5):
+                message(kind, c, u).wait_recv()
+            rows = piece(u)
+
+            def ring_sum(pair):
+                return (
+                    own[c, pair, rows]
+                    + from_left[c, pair, rows].astype(F32)
+                    + from_right[c, pair, rows].astype(F32)
+                )
+
+            to_pair[c, rows] = ring_sum(1 - pair_at).astype(BF16)
+            message(6, c, u).start()
+            mine[c, rows] = ring_sum(pair_at)
 
     def row_copy(chunk, p):
         return remote(
             ssend.at[chunk], srow.at[chunk, mt], row_send.at[chunk, p], row_recv.at[chunk, mt], {TEN: p}
         )
 
-    for chunk in range(chunks):
-
+    def end_pair(c):
+        squares = []
+        for u in pieces:
+            message(6, c, u).wait_recv()
+            rows = piece(u)
+            square = jnp.zeros((PIECE, LANES), F32)
+            for i in range(share // LANES):
+                lane = pl.ds(i * LANES, LANES)
+                s = mine[c, rows, lane] + from_pair[c, rows, lane].astype(F32)
+                mine[c, rows, lane] = s
+                square = square + s * s
+            squares.append(jnp.sum(square, axis=1, keepdims=True))
+        sums = jnp.concatenate(squares, axis=0)
+        ssend[c] = jnp.broadcast_to(sums, (LANES, LANES)).T[:8]
+        srow[c, mt] = ssend[c]
+
+        @pl.loop(0, nt - 1)
+        def _(j):
+            row_copy(c, partner(j, mt, nt)).start()
+
+    def normalize(c):
         @pl.loop(0, nt - 1)
         def _(j):
             p = partner(j, mt, nt)
-            slot = precv.at[p, rows_of(chunk), :]
-            pltpu.make_async_copy(slot, slot, part_recv.at[chunk, p]).wait()
-
-        here = rows_of(chunk)
-        squares = jnp.zeros((TOKENS_PER_PART, LANES), F32)
-        for c in range(share // LANES):
-            lane = pl.ds(c * LANES, LANES)
-            s = precv[0, here, lane].astype(F32)
-            for g in range(1, nt):
-                s = s + precv[g, here, lane].astype(F32)
-            total[here, lane] = s
-            squares = squares + s * s
-        sums = jnp.sum(squares, axis=1, keepdims=True)
-        ssend[chunk] = jnp.broadcast_to(sums, (TOKENS_PER_PART, LANES)).T[:8]
-        srow[chunk, mt] = ssend[chunk]
-
-        @pl.loop(0, nt - 1)
-        def _(j):
-            row_copy(chunk, partner(j, mt, nt)).start()
-
-    for chunk in range(chunks):
-
-        @pl.loop(0, nt - 1)
-        def _(j):
-            p = partner(j, mt, nt)
-            slot = srow.at[chunk, p]
-            pltpu.make_async_copy(slot, slot, row_recv.at[chunk, p]).wait()
-
-        here = rows_of(chunk)
-        s = srow[chunk, 0]
+            slot = srow.at[c, p]
+            pltpu.make_async_copy(slot, slot, row_recv.at[c, p]).wait()
+
+        s = srow[c, 0]
         for g in range(1, nt):
-            s = s + srow[chunk, g]
+            s = s + srow[c, g]
         scale = lax.rsqrt(s * (1.0 / (share * nt)) + 1e-06)
-        scale = jnp.broadcast_to(scale[:1], (LANES, TOKENS_PER_PART)).T
-        for c in range(share // LANES):
-            lane = pl.ds(c * LANES, LANES)
-            out[here, lane] = (total[here, lane] * scale * gain[:, lane]).astype(BF16)
-
-    @pl.when(me < nc - 1)
-    def _():
-        for copy in halos:
-            copy.wait_send()
-
-    @pl.loop(0, nc - 1)
-    def _(j):
-        p = partner(j, me, nc)
-        filter_copy(p).wait_send()
-        for part in range(parts):
-            signal_copy(part, p).wait_send()
-            conv_copy(part, p).wait_send()
-
-    @pl.loop(0, nt - 1)
-    def _(j):
-        p = partner(j, mt, nt)
-        for chunk in range(chunks):
-            part_copy(chunk, p).wait_send()
-            row_copy(chunk, p).wait_send()
+        scale = jnp.broadcast_to(scale[:1], (LANES, LANES)).T
+        for i in range(share // LANES):
+            lane = pl.ds(i * LANES, LANES)
+            out[rows_of(c), lane] = (mine[c, :, lane] * scale * gain[:, lane]).astype(BF16)
+
+    gate(0)
+    loads[5].wait()
+    start_ring(0)
+    pass_on(0)
+    gate(1)
+    start_ring(1)
+    end_ring(0)
+    pass_on(1)
+    end_pair(0)
+    end_ring(1)
+    normalize(0)
+    end_pair(1)
+    normalize(1)
+
+    settle(9)
 
 
 def per_device(
@@ -562,7 +646,7 @@
     parts = per // PART
     blocks = nc * (tokens // LANES)
     outer = blocks // INNER
-    chunks = tokens // TOKENS_PER_PART
+    halves = tokens // LANES
     fwd, bwd, twist = (jnp.asarray(x) for x in tables(blocks))
     anywhere = pl.BlockSpec(memory_space=pl.ANY)
     vmem = pl.BlockSpec(memory_space=pltpu.VMEM)
@@ -592,11 +676,13 @@
             pltpu.VMEM((parts, blocks * PART, 2 * LANES), F32),
             pltpu.VMEM((blocks * PART, 2 * LANES), F32),
             pltpu.VMEM((tokens, width), BF16),
-            pltpu.VMEM((nt, tokens, share), BF16),
-            pltpu.VMEM((nt, tokens, share), BF16),
-            pltpu.VMEM((tokens, share), F32),
-            pltpu.VMEM((chunks, 8, TOKENS_PER_PART), F32),
-            pltpu.VMEM((chunks, nt, 8, TOKENS_PER_PART), F32),
+            *[pltpu.VMEM((halves, 2, LANES, share), BF16)] * 6,
+            pltpu.VMEM((halves, 2, LANES, share), F32),
+            pltpu.VMEM((halves, LANES, share), BF16),
+            pltpu.VMEM((halves, LANES, share), BF16),
+            pltpu.VMEM((halves, LANES, share), F32),
+            pltpu.VMEM((halves, 8, LANES), F32),
+            pltpu.VMEM((halves, nt, 8, LANES), F32),
             dma((6,)),
             dma((3,)),
             dma((3,)),
@@ -604,12 +690,12 @@
             dma((nc,)),
             dma((parts, nc)),
             dma((parts, nc)),
-            dma((parts, nc)),
-            dma((parts, nc)),
-            dma((chunks, nt)),
-            dma((chunks, nt)),
-            dma((chunks, nt)),
-            dma((chunks, nt)),
+            dma((parts + halves - 1, nc)),
+            dma((parts + halves - 1, nc)),
+            dma((7, halves, LANES // PIECE)),
+            dma((7, halves, LANES // PIECE)),
+            dma((halves, nt)),
+            dma((halves, nt)),
         ],
         compiler_params=pltpu.CompilerParams(
             collective_id=0, has_side_effects=True, vmem_limit_bytes=56 * 1024 * 1024

time: 96.4 us -> 86.2 us (0.89); the launches traced: 96.2 us -> 85 us
  Pallas kernels: 94.5 us -> 83.3 us
    pallas_call x1, Pallas kernels: 94.5 us -> 83.3 us  [per_device(): pl.pallas_call(functools.partial(kernel, nc, nt), out_shape=jax.ShapeDtyp...]
where the time goes in v2:
time: 86.2 us; the launch traced here: 85 us
  Pallas kernels  83.3 us (97%)
  local copies, waits for them, and re-layouts  1.67 us (2%)
    pallas_call x1, Pallas kernels, per_device(): pl.pallas_call(functools.partial(kernel, nc, nt), out_shape=jax.ShapeDtyp...  83.3 us

profile of v2, /device:TPU:8, one launch (start us, length us, event | category | flops | bytes accessed | tf_op | source)
XLA Modules:
  0.0 85.0 jit_solution(3295596333090220369)
XLA Ops:
  0.0 83.3 %shard_map.109 = bf16[256,512]{1,0:T(8,128)(2,1)} custom-call(bf16[256,1024]{1,0:T(8,128)(2,1)} %q_hbm.1, bf16[256,1024]{1,0:T(8,128)(2,1)} %k_hbm.1, bf16[256,1024]{1,0:T(8,128)(2,1)} %v_hbm.1, bf16[1024,256]{1,0:T(8,128)(2,1)} %filt_hbm.1, bf16[1024,4096]{1,0:T(8,128)(2,1)} %w_hbm.1, bf16[2,256,256]{2,1,0:T(8,128)(2,1)} %constant.6.clone.fwd_hbm, ...), custom_call_target="tpu_custom_call" | custom-call | tf_op jit(solution)/shard_map/pallas_call | solution.py:654
  83.4 1.7 %copy.13 = bf16[256,512]{1,0:T(8,128)(2,1)} copy(bf16[256,512]{1,0:T(8,128)(2,1)} %shard_map.109) | data formatting | bytes 524288

commit v3 on v2

--- a/solution.py
+++ b/solution.py
@@ -120,11 +120,15 @@
     w_hbm,
     fwd_hbm,
     bwd_hbm,
+    taps_hbm,
+    skip_hbm,
+    gain_hbm,
+    twist_hbm,
+    out,
     taps,
     skip,
     gain,
     twist,
-    out,
     qbuf,
     kbuf,
     vbuf,
@@ -195,6 +199,16 @@
             device_id_type=pl.DeviceIdType.MESH,
         )
 
+    barrier = pltpu.get_barrier_semaphore()
+
+    @pl.loop(0, nc - 1)
+    def _(j):
+        pl.semaphore_signal(barrier, inc=1, device_id={CTX: partner(j, me, nc)})
+
+    @pl.loop(0, nt - 1)
+    def _(j):
+        pl.semaphore_signal(barrier, inc=1, device_id={TEN: partner(j, mt, nt)})
+
     body = pl.ds(HALO, tokens)
     loads = [
         pltpu.make_async_copy(src, dst, load_sem.at[i])
@@ -206,21 +220,15 @@
                 (fwd_hbm, fwd),
                 (bwd_hbm, bwd),
                 (w_hbm, wbuf),
+                (taps_hbm, taps),
+                (twist_hbm, twist),
+                (skip_hbm, skip),
+                (gain_hbm, gain),
             )
         )
     ]
-    for copy in loads:
-        copy.start()
-
-    barrier = pltpu.get_barrier_semaphore()
-
-    @pl.loop(0, nc - 1)
-    def _(j):
-        pl.semaphore_signal(barrier, inc=1, device_id={CTX: partner(j, me, nc)})
-
-    @pl.loop(0, nt - 1)
-    def _(j):
-        pl.semaphore_signal(barrier, inc=1, device_id={TEN: partner(j, mt, nt)})
+    for i in (6, 0, 1, 2, 7, 3, 4, 8, 9, 5):
+        loads[i].start()
 
     pl.semaphore_wait(barrier, nc - 1 + nt - 1)
 
@@ -308,7 +316,7 @@
         col = pl.multiple_of(i % columns * LANES, LANES)
         return row, col
 
-    for i in (0, 1):
+    for i in (6, 0, 1):
         loads[i].wait()
 
     @pl.when(me > 0)
@@ -399,7 +407,7 @@
     def _(s):
         pltpu.make_async_copy(frecv.at[s], frecv.at[s], filt_recv.at[s]).wait()
 
-    for i in (3, 4):
+    for i in (3, 4, 7):
         loads[i].wait()
 
     @pl.loop(0, parts)
@@ -543,11 +551,9 @@
             message(0, c, u).start()
             message(1, c, u).start()
         terms(c, ring_at + 1, to_right)
-        for u in pieces:
-            message(2, c, u).start()
+        message(2, c, 0).start()
         terms(c, ring_at + RING - 1, to_left)
-        for u in pieces:
-            message(3, c, u).start()
+        message(3, c, 0).start()
         terms(c, ring_at, own)
 
     def pass_on(c):
@@ -559,6 +565,9 @@
                         buf[c, pair, rows].astype(F32) + relay[c, pair, rows].astype(F32)
                     ).astype(BF16)
                 message(kind + 4, c, u).start()
+            if u + 1 < len(pieces):
+                message(2, c, u + 1).start()
+                message(3, c, u + 1).start()
 
     def end_ring(c):
         for u in pieces:
@@ -618,6 +627,7 @@
             lane = pl.ds(i * LANES, LANES)
             out[rows_of(c), lane] = (mine[c, :, lane] * scale * gain[:, lane]).astype(BF16)
 
+    loads[8].wait()
     gate(0)
     loads[5].wait()
     start_ring(0)
@@ -628,6 +638,7 @@
     pass_on(1)
     end_pair(0)
     end_ring(1)
+    loads[9].wait()
     normalize(0)
     end_pair(1)
     normalize(1)
@@ -653,10 +664,14 @@
     dma = pltpu.SemaphoreType.DMA
     return pl.pallas_call(
         functools.partial(kernel, nc, nt),
-        out_shape=jax.ShapeDtypeStruct((tokens, share), BF16),
-        in_specs=[anywhere] * 7 + [vmem] * 4,
+        out_shape=pltpu.VMEM((tokens, share), BF16),
+        in_specs=[anywhere] * 11,
         out_specs=vmem,
         scratch_shapes=[
+            pltpu.VMEM(short_taps.shape, F32),
+            pltpu.VMEM((1, width), F32),
+            pltpu.VMEM((1, share), F32),
+            pltpu.VMEM(twist.shape, F32),
             pltpu.VMEM((tokens + HALO, width), BF16),
             pltpu.VMEM((tokens + HALO, width), BF16),
             pltpu.VMEM((tokens + HALO, width), BF16),
@@ -683,7 +698,7 @@
             pltpu.VMEM((halves, LANES, share), F32),
             pltpu.VMEM((halves, 8, LANES), F32),
             pltpu.VMEM((halves, nt, 8, LANES), F32),
-            dma((6,)),
+            dma((10,)),
             dma((3,)),
             dma((3,)),
             dma((nc,)),

time: 86.2 us -> 83.6 us (0.970)
  Pallas kernels: 83.3 us -> 81.8 us
  local copies, waits for them, and re-layouts: 1.67 us -> 0.71 us
    pallas_call x1, Pallas kernels: 83.3 us -> 81.8 us  [per_device(): pl.pallas_call(functools.partial(kernel, nc, nt), out_shape=pltpu.VMEM((t...]
    unnamed x1, local copies, waits for them, and re-layouts: 1.67 us -> 0.71 us
where the time goes in v3:
time: 83.6 us; the launch traced here: 82.5 us
  Pallas kernels  81.8 us (98%)
    pallas_call x1, Pallas kernels, per_device(): pl.pallas_call(functools.partial(kernel, nc, nt), out_shape=pltpu.VMEM((t...  81.8 us

profile of v3, /device:TPU:8, one launch (start us, length us, event | category | flops | bytes accessed | tf_op | source)
XLA Modules:
  0.0 82.5 jit_solution(13595554669114846412)
XLA Ops:
  0.0 81.8 %shard_map.109 = bf16[256,512]{1,0:T(8,128)(2,1)S(1)} custom-call(bf16[256,1024]{1,0:T(8,128)(2,1)} %q_hbm.1, bf16[256,1024]{1,0:T(8,128)(2,1)} %k_hbm.1, bf16[256,1024]{1,0:T(8,128)(2,1)} %v_hbm.1, bf16[1024,256]{1,0:T(8,128)(2,1)} %filt_hbm.1, bf16[1024,4096]{1,0:T(8,128)(2,1)} %w_hbm.1, bf16[2,256,256]{2,1,0:T(8,128)(2,1)} %constant.6.clone.fwd_hbm, ...), custom_call_target="tpu_custom_call" | custom-call | tf_op jit(solution)/shard_map/pallas_call | solution.py:665
  81.8 0.7 copy.13

commit v4 on v3

--- a/solution.py
+++ b/solution.py
@@ -18,7 +18,7 @@
 SHIFT = 0.25
 INNER = 8
 RING = 4
-PIECE = 64
+PIECE = LANES // 2
 
 
 def times(z, c):
@@ -148,15 +148,16 @@
     fspec,
     dspec,
     gated,
-    far,
-    relay,
-    to_right,
-    to_left,
-    from_left,
-    from_right,
-    own,
-    to_pair,
-    from_pair,
+    xsend,
+    xrecv,
+    xown,
+    ysend,
+    yrecv,
+    yown,
+    yxsend,
+    yxrecv,
+    xysend,
+    xyrecv,
     mine,
     ssend,
     srow,
@@ -201,11 +202,11 @@
 
     barrier = pltpu.get_barrier_semaphore()
 
-    @pl.loop(0, nc - 1)
+    @pl.loop(0, nc - 1, unroll=True)
     def _(j):
         pl.semaphore_signal(barrier, inc=1, device_id={CTX: partner(j, me, nc)})
 
-    @pl.loop(0, nt - 1)
+    @pl.loop(0, nt - 1, unroll=True)
     def _(j):
         pl.semaphore_signal(barrier, inc=1, device_id={TEN: partner(j, mt, nt)})
 
@@ -227,7 +228,7 @@
             )
         )
     ]
-    for i in (6, 0, 1, 2, 7, 3, 4, 8, 9, 5):
+    for i in (0, 1, 6):
         loads[i].start()
 
     pl.semaphore_wait(barrier, nc - 1 + nt - 1)
@@ -246,14 +247,13 @@
                 for part in range(parts):
                     signal_copy(part, p).wait_send()
             if stage > 4:
-                for group in range(parts + halves - 1):
+                for group in range(parts, parts + halves - 1):
                     conv_copy(group, p).wait_send()
 
         if stage > 6:
             for c in range(halves):
-                for u in pieces:
-                    for kind in range(7):
-                        message(kind, c, u).wait_send()
+                for kind, d in messages:
+                    message(kind, c, d).wait_send()
 
             @pl.loop(0, nt - 1)
             def _(j):
@@ -290,7 +290,7 @@
             {CTX: p},
         )
 
-    @pl.loop(0, nc - 1)
+    @pl.loop(0, nc - 1, unroll=True)
     def _(j):
         filter_copy(partner(j, me, nc)).start()
 
@@ -298,6 +298,8 @@
         filt_hbm.at[pl.ds(pl.multiple_of(me * per, PART), per), :], frecv.at[me], filt_recv.at[me]
     )
     own_filter.start()
+    for i in (2, 7, 3, 4, 8, 9, 5):
+        loads[i].start()
 
     def feature(buf, r, row, lane):
         wide = buf[pl.ds(row, LANES + HALO), lane].astype(F32)[HALO - 8 :]
@@ -343,7 +345,7 @@
 
     for part in range(parts):
 
-        @pl.loop(0, nc - 1)
+        @pl.loop(0, nc - 1, unroll=True)
         def _(j):
             signal_copy(part, partner(j, me, nc)).start()
 
@@ -489,6 +491,11 @@
 
         send_conv(part)
 
+    @pl.loop(0, nc - 1)
+    def _(j):
+        for group in range(parts):
+            conv_copy(group, partner(j, me, nc)).wait_send()
+
     for half in range(1, halves):
         send_conv(parts + half - 1)
 
@@ -509,105 +516,105 @@
         return pl.ds(chunk * LANES, LANES)
 
     ring_at, pair_at = mt % RING, mt // RING
-    rightward = {TEN: pair_at * RING + (ring_at + 1) % RING}
-    leftward = {TEN: pair_at * RING + (ring_at + RING - 1) % RING}
     across = {TEN: (1 - pair_at) * RING + ring_at}
 
     def term(chunk, pair, ring):
         column = pl.multiple_of((pair * RING + ring) * share, LANES)
         return jnp.dot(gated[rows_of(chunk), :], wbuf[:, pl.ds(column, share)], preferred_element_type=F32)
 
-    def terms(chunk, ring, into):
-        @pl.loop(0, 2)
-        def _(pair):
-            into[chunk, pair] = term(chunk, pair, ring % RING).astype(into.dtype)
-
-    def piece(u):
-        return pl.ds(u * PIECE, PIECE)
-
-    def first(u):
-        return pl.ds(u * PIECE, PIECE // 2)
-
-    def second(u):
-        return pl.ds(u * PIECE + PIECE // 2, PIECE // 2)
-
-    def message(kind, c, u):
-        src, dst, device = (
-            lambda: (far.at[c, :, first(u)], relay.at[c, :, first(u)], rightward),
-            lambda: (far.at[c, :, second(u)], relay.at[c, :, second(u)], leftward),
-            lambda: (to_right.at[c, :, second(u)], from_left.at[c, :, second(u)], rightward),
-            lambda: (to_left.at[c, :, first(u)], from_right.at[c, :, first(u)], leftward),
-            lambda: (to_right.at[c, :, first(u)], from_left.at[c, :, first(u)], rightward),
-            lambda: (to_left.at[c, :, second(u)], from_right.at[c, :, second(u)], leftward),
-            lambda: (to_pair.at[c, piece(u)], from_pair.at[c, piece(u)], across),
-        )[kind]()
-        return remote(src, dst, red_send.at[kind, c, u], red_recv.at[kind, c, u], device)
-
-    pieces = range(LANES // PIECE)
-
-    def start_ring(c):
-        terms(c, ring_at + 2, far)
-        for u in pieces:
-            message(0, c, u).start()
-            message(1, c, u).start()
-        terms(c, ring_at + 1, to_right)
-        message(2, c, 0).start()
-        terms(c, ring_at + RING - 1, to_left)
-        message(3, c, 0).start()
-        terms(c, ring_at, own)
-
-    def pass_on(c):
-        for u in pieces:
-            for kind, rows, buf in ((0, first(u), to_right), (1, second(u), to_left)):
-                message(kind, c, u).wait_recv()
-                for pair in range(2):
-                    buf[c, pair, rows] = (
-                        buf[c, pair, rows].astype(F32) + relay[c, pair, rows].astype(F32)
-                    ).astype(BF16)
-                message(kind + 4, c, u).start()
-            if u + 1 < len(pieces):
-                message(2, c, u + 1).start()
-                message(3, c, u + 1).start()
-
-    def end_ring(c):
-        for u in pieces:
-            for kind in (2, 3, 4, 5):
-                message(kind, c, u).wait_recv()
-            rows = piece(u)
-
-            def ring_sum(pair):
-                return (
-                    own[c, pair, rows]
-                    + from_left[c, pair, rows].astype(F32)
-                    + from_right[c, pair, rows].astype(F32)
-                )
-
-            to_pair[c, rows] = ring_sum(1 - pair_at).astype(BF16)
-            message(6, c, u).start()
-            mine[c, rows] = ring_sum(pair_at)
+    upper, lower = pl.ds(0, PIECE), pl.ds(PIECE, PIECE)
+    further = (2, 1, 3)
+
+    def ring_device(d):
+        return {TEN: pair_at * RING + (ring_at + d) % RING}
+
+    def message(kind, c, d):
+        src, dst, device = {
+            "far": lambda: (xsend.at[c, 0, d], xrecv.at[c, 0, d], ring_device(d)),
+            "near": lambda: (xsend.at[c, 1, d], xrecv.at[c, 1, d], ring_device(d)),
+            "pair": lambda: (ysend.at[c, d], yrecv.at[c, d], across),
+            "then_ring": lambda: (yxsend.at[c, d], yxrecv.at[c, d], ring_device(d)),
+            "then_pair": lambda: (xysend.at[c], xyrecv.at[c], across),
+        }[kind]()
+        k = ("far", "near", "pair", "then_ring", "then_pair").index(kind)
+        return remote(src, dst, red_send.at[k, c, d], red_recv.at[k, c, d], device)
+
+    messages = [
+        (kind, d)
+        for kind, ds in (
+            ("far", further),
+            ("near", further),
+            ("pair", (0, 1, 2, 3)),
+            ("then_ring", further),
+            ("then_pair", (0,)),
+        )
+        for d in ds
+    ]
+
+    def start_sums(c):
+        for d in (*further, 0):
+            t = term(c, 1 - pair_at, (ring_at + d) % RING)
+            ysend[c, d] = t[PIECE:].astype(BF16)
+            message("pair", c, d).start()
+            if d:
+                xsend[c, 0, d] = t[:PIECE].astype(BF16)
+                message("far", c, d).start()
+            else:
+                xown[c, 0] = t[:PIECE]
+        for d in (*further, 0):
+            t = term(c, pair_at, (ring_at + d) % RING)
+            yown[c, d] = t[PIECE:]
+            if d:
+                xsend[c, 1, d] = t[:PIECE].astype(BF16)
+                message("near", c, d).start()
+            else:
+                xown[c, 1] = t[:PIECE]
+
+    def turn_corner(c):
+        for d in further:
+            message("far", c, d).wait_recv()
+        s = xown[c, 0]
+        for d in further:
+            s = s + xrecv[c, 0, d].astype(F32)
+        xysend[c] = s.astype(BF16)
+        message("then_pair", c, 0).start()
+        for d in further:
+            message("pair", c, d).wait_recv()
+            yxsend[c, d] = (yown[c, d] + yrecv[c, d].astype(F32)).astype(BF16)
+            message("then_ring", c, d).start()
 
     def row_copy(chunk, p):
         return remote(
             ssend.at[chunk], srow.at[chunk, mt], row_send.at[chunk, p], row_recv.at[chunk, mt], {TEN: p}
         )
 
-    def end_pair(c):
+    def end_sums(c):
         squares = []
-        for u in pieces:
-            message(6, c, u).wait_recv()
-            rows = piece(u)
+
+        def finish(rows, parts_of):
             square = jnp.zeros((PIECE, LANES), F32)
             for i in range(share // LANES):
                 lane = pl.ds(i * LANES, LANES)
-                s = mine[c, rows, lane] + from_pair[c, rows, lane].astype(F32)
+                s = parts_of[0][:, lane]
+                for ref in parts_of[1:]:
+                    s = s + ref[:, lane].astype(F32)
                 mine[c, rows, lane] = s
                 square = square + s * s
             squares.append(jnp.sum(square, axis=1, keepdims=True))
+
+        for d in further:
+            message("near", c, d).wait_recv()
+        message("then_pair", c, 0).wait_recv()
+        finish(upper, [xown.at[c, 1], *(xrecv.at[c, 1, d] for d in further), xyrecv.at[c]])
+        message("pair", c, 0).wait_recv()
+        for d in further:
+            message("then_ring", c, d).wait_recv()
+        finish(lower, [yown.at[c, 0], yrecv.at[c, 0], *(yxrecv.at[c, d] for d in further)])
         sums = jnp.concatenate(squares, axis=0)
         ssend[c] = jnp.broadcast_to(sums, (LANES, LANES)).T[:8]
         srow[c, mt] = ssend[c]
 
-        @pl.loop(0, nt - 1)
+        @pl.loop(0, nt - 1, unroll=True)
         def _(j):
             row_copy(c, partner(j, mt, nt)).start()
 
@@ -630,17 +637,15 @@
     loads[8].wait()
     gate(0)
     loads[5].wait()
-    start_ring(0)
-    pass_on(0)
+    start_sums(0)
     gate(1)
-    start_ring(1)
-    end_ring(0)
-    pass_on(1)
-    end_pair(0)
-    end_ring(1)
+    start_sums(1)
+    turn_corner(0)
+    turn_corner(1)
+    end_sums(0)
+    end_sums(1)
     loads[9].wait()
     normalize(0)
-    end_pair(1)
     normalize(1)
 
     settle(9)
@@ -691,10 +696,16 @@
             pltpu.VMEM((parts, blocks * PART, 2 * LANES), F32),
             pltpu.VMEM((blocks * PART, 2 * LANES), F32),
             pltpu.VMEM((tokens, width), BF16),
-            *[pltpu.VMEM((halves, 2, LANES, share), BF16)] * 6,
-            pltpu.VMEM((halves, 2, LANES, share), F32),
-            pltpu.VMEM((halves, LANES, share), BF16),
-            pltpu.VMEM((halves, LANES, share), BF16),
+            pltpu.VMEM((halves, 2, RING, PIECE, share), BF16),
+            pltpu.VMEM((halves, 2, RING, PIECE, share), BF16),
+            pltpu.VMEM((halves, 2, PIECE, share), F32),
+            pltpu.VMEM((halves, RING, PIECE, share), BF16),
+            pltpu.VMEM((halves, RING, PIECE, share), BF16),
+            pltpu.VMEM((halves, RING, PIECE, share), F32),
+            pltpu.VMEM((halves, RING, PIECE, share), BF16),
+            pltpu.VMEM((halves, RING, PIECE, share), BF16),
+            pltpu.VMEM((halves, PIECE, share), BF16),
+            pltpu.VMEM((halves, PIECE, share), BF16),
             pltpu.VMEM((halves, LANES, share), F32),
             pltpu.VMEM((halves, 8, LANES), F32),
             pltpu.VMEM((halves, nt, 8, LANES), F32),
@@ -707,8 +718,8 @@
             dma((parts, nc)),
             dma((parts + halves - 1, nc)),
             dma((parts + halves - 1, nc)),
-            dma((7, halves, LANES // PIECE)),
-            dma((7, halves, LANES // PIECE)),
+            dma((5, halves, RING)),
+            dma((5, halves, RING)),
             dma((halves, nt)),
             dma((halves, nt)),
         ],

time: 83.6 us -> 80.2 us (0.959)
  Pallas kernels: 81.8 us -> 78.7 us
    pallas_call x1, Pallas kernels: 81.8 us -> 78.7 us  [per_device(): pl.pallas_call(functools.partial(kernel, nc, nt), out_shape=pltpu.VMEM((t...]
where the time goes in v4:
time: 80.2 us; the launch traced here: 79.4 us
  Pallas kernels  78.7 us (98%)
    pallas_call x1, Pallas kernels, per_device(): pl.pallas_call(functools.partial(kernel, nc, nt), out_shape=pltpu.VMEM((t...  78.7 us

profile of v4, /device:TPU:8, one launch (start us, length us, event | category | flops | bytes accessed | tf_op | source)
XLA Modules:
  0.0 79.4 jit_solution(7605419893790962779)
XLA Ops:
  0.0 78.7 %shard_map.109 = bf16[256,512]{1,0:T(8,128)(2,1)S(1)} custom-call(bf16[256,1024]{1,0:T(8,128)(2,1)} %q_hbm.1, bf16[256,1024]{1,0:T(8,128)(2,1)} %k_hbm.1, bf16[256,1024]{1,0:T(8,128)(2,1)} %v_hbm.1, bf16[1024,256]{1,0:T(8,128)(2,1)} %filt_hbm.1, bf16[1024,4096]{1,0:T(8,128)(2,1)} %w_hbm.1, bf16[2,256,256]{2,1,0:T(8,128)(2,1)} %constant.6.clone.fwd_hbm, ...), custom_call_target="tpu_custom_call" | custom-call | tf_op jit(solution)/shard_map/pallas_call | solution.py:670
  78.7 0.7 copy.13

commit v5 on v4

--- a/solution.py
+++ b/solution.py
@@ -16,6 +16,7 @@
 LANES = 128
 PART = 16
 SHIFT = 0.25
+GROUP = 2
 INNER = 8
 RING = 4
 PIECE = LANES // 2
@@ -247,7 +248,7 @@
                 for part in range(parts):
                     signal_copy(part, p).wait_send()
             if stage > 4:
-                for group in range(parts, parts + halves - 1):
+                for group in range(parts + halves - 1):
                     conv_copy(group, p).wait_send()
 
         if stage > 6:
@@ -367,8 +368,14 @@
         lane = pl.ds(col, LANES)
         qfeat[pl.ds(row, LANES), lane] = feature(qbuf, 0, row, lane)
 
-    def block_of(k1):
-        return pl.ds(k1 * PART, PART)
+    def row_at(q, r):
+        return (q * INNER + r) * PART
+
+    together = min(GROUP, outer)
+    groups = [range(q, q + together) for q in range(0, outer, together)]
+
+    def group_rows(qs):
+        return pl.ds(row_at(qs[0], 0), together * INNER * PART)
 
     left, right = pl.ds(0, LANES), pl.ds(LANES, LANES)
 
@@ -384,12 +391,27 @@
                 re, im = times(z, turn(-b * (q + SHIFT) / blocks))
                 mid[b, q, 0] = re
                 mid[b, q, 1] = jnp.zeros_like(re) if im is None else im
-        for q in range(outer):
+
+    def inner_forward(qs):
+        for q in qs:
             y = [(mid[b, q, 0], mid[b, q, 1]) for b in range(INNER)]
             for r, (re, im) in enumerate(dft(y, -1)):
                 k1 = q + outer * r
                 cos, sin = twist[0, pl.ds(k1, 1), :], twist[1, pl.ds(k1, 1), :]
-                put(k1 * PART, re * cos - im * sin, im * cos + re * sin)
+                put(row_at(q, r), re * cos - im * sin, im * cos + re * sin)
+
+    def inner_backward(qs):
+        for q in qs:
+            y = []
+            for r in range(INNER):
+                k1, rows = q + outer * r, pl.ds(row_at(q, r), PART)
+                cos, sin = twist[0, pl.ds(k1, 1), :], twist[1, pl.ds(k1, 1), :]
+                re, im = dspec[rows, left], dspec[rows, right]
+                y.append((re * cos + im * sin, im * cos - re * sin))
+            for b, z in enumerate(dft(y, 1)):
+                re, im = times(z, turn(b * (q + SHIFT) / blocks))
+                mid[b, q, 0] = re
+                mid[b, q, 1] = im
 
     def put(row, re, im):
         rows = pl.ds(row, re.shape[0])
@@ -403,8 +425,6 @@
         dot = functools.partial(jnp.dot, preferred_element_type=F32)
         return dot(a, table[0]) + dot(b, table[0]) + dot(a, table[1])
 
-    tall = min(256, blocks * PART)
-
     @pl.loop(0, nc)
     def _(s):
         pltpu.make_async_copy(frecv.at[s], frecv.at[s], filt_recv.at[s]).wait()
@@ -415,11 +435,9 @@
     @pl.loop(0, parts)
     def _(part):
         outer_forward(frecv, part)
-
-        @pl.loop(0, blocks * PART // tall)
-        def _(i):
-            rows = pl.ds(pl.multiple_of(i * tall, tall), tall)
-            fspec[part, rows, :] = product(rows, fwd)
+        for qs in groups:
+            inner_forward(qs)
+            fspec[part, group_rows(qs), :] = product(group_rows(qs), fwd)
 
     def conv_slice(group, p):
         if isinstance(group, int) and group >= parts:
@@ -460,27 +478,16 @@
 
         outer_forward(srecv, part)
 
-        @pl.loop(0, blocks * PART // tall)
-        def _(i):
-            start = pl.multiple_of(i * tall, tall)
-            rows = pl.ds(start, tall)
+        for qs in groups:
+            rows = group_rows(qs)
+            inner_forward(qs)
             spec = product(rows, fwd)
             re, im = spec[:, :LANES], spec[:, LANES:]
             fre, fim = fspec[part, rows, left], fspec[part, rows, right]
-            put(start, re * fre - im * fim, re * fim + im * fre)
+            put(row_at(qs[0], 0), re * fre - im * fim, re * fim + im * fre)
             dspec[rows, :] = product(rows, bwd)
-
-        for q in range(outer):
-            y = []
-            for r in range(INNER):
-                k1 = q + outer * r
-                cos, sin = twist[0, pl.ds(k1, 1), :], twist[1, pl.ds(k1, 1), :]
-                re, im = dspec[block_of(k1), left], dspec[block_of(k1), right]
-                y.append((re * cos + im * sin, im * cos - re * sin))
-            for b, z in enumerate(dft(y, 1)):
-                re, im = times(z, turn(b * (q + SHIFT) / blocks))
-                mid[b, q, 0] = re
-                mid[b, q, 1] = im
+            inner_backward(qs)
+
         for b in range(INNER):
             lane = pl.ds(b % halves * LANES, LANES)
             y = [(mid[b, q, 0], mid[b, q, 1]) for q in range(outer)]
@@ -490,11 +497,6 @@
                 ).astype(BF16)
 
         send_conv(part)
-
-    @pl.loop(0, nc - 1)
-    def _(j):
-        for group in range(parts):
-            conv_copy(group, partner(j, me, nc)).wait_send()
 
     for half in range(1, halves):
         send_conv(parts + half - 1)

time: 80.2 us -> 77.9 us (0.971)
  Pallas kernels: 78.7 us -> 77.1 us
    pallas_call x1, Pallas kernels: 78.7 us -> 77.1 us  [per_device(): pl.pallas_call(functools.partial(kernel, nc, nt), out_shape=pltpu.VMEM((t...]
where the time goes in v5:
time: 77.9 us; the launch traced here: 77.8 us
  Pallas kernels  77.1 us (99%)
    pallas_call x1, Pallas kernels, per_device(): pl.pallas_call(functools.partial(kernel, nc, nt), out_shape=pltpu.VMEM((t...  77.1 us

profile of v5, /device:TPU:8, one launch (start us, length us, event | category | flops | bytes accessed | tf_op | source)
XLA Modules:
  0.0 77.8 jit_solution(13557317733982120600)
XLA Ops:
  0.0 77.1 %shard_map.109 = bf16[256,512]{1,0:T(8,128)(2,1)S(1)} custom-call(bf16[256,1024]{1,0:T(8,128)(2,1)} %q_hbm.1, bf16[256,1024]{1,0:T(8,128)(2,1)} %k_hbm.1, bf16[256,1024]{1,0:T(8,128)(2,1)} %v_hbm.1, bf16[1024,256]{1,0:T(8,128)(2,1)} %filt_hbm.1, bf16[1024,4096]{1,0:T(8,128)(2,1)} %w_hbm.1, bf16[2,256,256]{2,1,0:T(8,128)(2,1)} %constant.6.clone.fwd_hbm, ...), custom_call_target="tpu_custom_call" | custom-call | tf_op jit(solution)/shard_map/pallas_call | solution.py:672
  77.1 0.7 copy.13

commit v6 on v5

--- a/solution.py
+++ b/solution.py
@@ -461,12 +461,6 @@
             conv_recv.at[group, me],
         ).start()
 
-    def await_conv(group):
-        @pl.loop(0, nc)
-        def _(s):
-            slot = crecv.at[conv_slice(group, s)]
-            pltpu.make_async_copy(slot, slot, conv_recv.at[group, s]).wait()
-
     @pl.loop(0, parts)
     def _(part):
         rows16 = pl.ds(pl.multiple_of(part * PART, PART), PART)
@@ -502,13 +496,17 @@
         send_conv(parts + half - 1)
 
     def gate(chunk):
-        for group in range(parts) if chunk == 0 else [parts + chunk - 1]:
-            await_conv(group)
         rows = rows_of(chunk)
+        sources = LANES // per
 
         @pl.loop(0, columns)
         def _(i):
-            lane = pl.ds(pl.multiple_of(i * LANES, LANES), LANES)
+            block = partner(i, me // sources, columns)
+            for n in range(sources):
+                for group in range(parts) if chunk == 0 else [parts + chunk - 1]:
+                    slot = crecv.at[conv_slice(group, block * sources + n)]
+                    pltpu.make_async_copy(slot, slot, conv_recv.at[group, block * sources + n]).wait()
+            lane = pl.ds(pl.multiple_of(block * LANES, LANES), LANES)
             conv = crecv[lane, rows].astype(F32).T
             gated[rows, lane] = (
                 qfeat[rows, lane] * (conv + skip[:, lane] * mixed[rows, lane].astype(F32))

time: 77.9 us -> 77.4 us (level)
  no operation moved by 1% of the time
where the time goes in v6:
time: 77.4 us; the launch traced here: 77.3 us
  Pallas kernels  76.6 us (99%)
    pallas_call x1, Pallas kernels, per_device(): pl.pallas_call(functools.partial(kernel, nc, nt), out_shape=pltpu.VMEM((t...  76.6 us

profile of v6, /device:TPU:8, one launch (start us, length us, event | category | flops | bytes accessed | tf_op | source)
XLA Modules:
  0.0 77.3 jit_solution(3401448463176497259)
XLA Ops:
  0.0 76.6 %shard_map.109 = bf16[256,512]{1,0:T(8,128)(2,1)S(1)} custom-call(bf16[256,1024]{1,0:T(8,128)(2,1)} %q_hbm.1, bf16[256,1024]{1,0:T(8,128)(2,1)} %k_hbm.1, bf16[256,1024]{1,0:T(8,128)(2,1)} %v_hbm.1, bf16[1024,256]{1,0:T(8,128)(2,1)} %filt_hbm.1, bf16[1024,4096]{1,0:T(8,128)(2,1)} %w_hbm.1, bf16[2,256,256]{2,1,0:T(8,128)(2,1)} %constant.6.clone.fwd_hbm, ...), custom_call_target="tpu_custom_call" | custom-call | tf_op jit(solution)/shard_map/pallas_call | solution.py:670
  76.6 0.7 copy.13

commit v7 on v6

--- a/solution.py
+++ b/solution.py
@@ -19,7 +19,7 @@
 GROUP = 2
 INNER = 8
 RING = 4
-PIECE = LANES // 2
+PIECE = 48
 
 
 def times(z, c):
@@ -234,7 +234,7 @@
 
     pl.semaphore_wait(barrier, nc - 1 + nt - 1)
 
-    def settle(stage):
+    def settle_inputs():
         @pl.when(me < nc - 1)
         def _():
             for copy in halos:
@@ -244,22 +244,25 @@
         def _(j):
             p = partner(j, me, nc)
             filter_copy(p).wait_send()
-            if stage > 2:
-                for part in range(parts):
-                    signal_copy(part, p).wait_send()
-            if stage > 4:
-                for group in range(parts + halves - 1):
-                    conv_copy(group, p).wait_send()
-
-        if stage > 6:
+            for part in range(parts):
+                signal_copy(part, p).wait_send()
+
+    def settle_conv():
+        @pl.loop(0, nc - 1)
+        def _(j):
+            for group in range(parts + halves - 1):
+                conv_copy(group, partner(j, me, nc)).wait_send()
+
+    def settle_sums():
+        for c in range(halves):
+            for kind, d in messages:
+                message(kind, c, d).wait_send()
+
+    def settle_rows():
+        @pl.loop(0, nt - 1)
+        def _(j):
             for c in range(halves):
-                for kind, d in messages:
-                    message(kind, c, d).wait_send()
-
-            @pl.loop(0, nt - 1)
-            def _(j):
-                for c in range(halves):
-                    row_copy(c, partner(j, mt, nt)).wait_send()
+                row_copy(c, partner(j, mt, nt)).wait_send()
 
     halos = [
         remote(
@@ -522,7 +525,7 @@
         column = pl.multiple_of((pair * RING + ring) * share, LANES)
         return jnp.dot(gated[rows_of(chunk), :], wbuf[:, pl.ds(column, share)], preferred_element_type=F32)
 
-    upper, lower = pl.ds(0, PIECE), pl.ds(PIECE, PIECE)
+    upper, lower = pl.ds(0, PIECE), pl.ds(PIECE, LANES - PIECE)
     further = (2, 1, 3)
 
     def ring_device(d):
@@ -551,7 +554,7 @@
         for d in ds
     ]
 
-    def start_sums(c):
+    def start_across(c):
         for d in (*further, 0):
             t = term(c, 1 - pair_at, (ring_at + d) % RING)
             ysend[c, d] = t[PIECE:].astype(BF16)
@@ -561,6 +564,8 @@
                 message("far", c, d).start()
             else:
                 xown[c, 0] = t[:PIECE]
+
+    def start_along(c):
         for d in (*further, 0):
             t = term(c, pair_at, (ring_at + d) % RING)
             yown[c, d] = t[PIECE:]
@@ -592,7 +597,7 @@
         squares = []
 
         def finish(rows, parts_of):
-            square = jnp.zeros((PIECE, LANES), F32)
+            square = jnp.zeros((rows.size, LANES), F32)
             for i in range(share // LANES):
                 lane = pl.ds(i * LANES, LANES)
                 s = parts_of[0][:, lane]
@@ -634,21 +639,26 @@
             lane = pl.ds(i * LANES, LANES)
             out[rows_of(c), lane] = (mine[c, :, lane] * scale * gain[:, lane]).astype(BF16)
 
+    settle_inputs()
     loads[8].wait()
     gate(0)
     loads[5].wait()
-    start_sums(0)
+    start_across(0)
+    start_along(0)
     gate(1)
-    start_sums(1)
+    start_across(1)
     turn_corner(0)
+    start_along(1)
     turn_corner(1)
+    settle_conv()
     end_sums(0)
     end_sums(1)
+    settle_sums()
     loads[9].wait()
     normalize(0)
     normalize(1)
 
-    settle(9)
+    settle_rows()
 
 
 def per_device(
@@ -699,11 +709,11 @@
             pltpu.VMEM((halves, 2, RING, PIECE, share), BF16),
             pltpu.VMEM((halves, 2, RING, PIECE, share), BF16),
             pltpu.VMEM((halves, 2, PIECE, share), F32),
-            pltpu.VMEM((halves, RING, PIECE, share), BF16),
-            pltpu.VMEM((halves, RING, PIECE, share), BF16),
-            pltpu.VMEM((halves, RING, PIECE, share), F32),
-            pltpu.VMEM((halves, RING, PIECE, share), BF16),
-            pltpu.VMEM((halves, RING, PIECE, share), BF16),
+            pltpu.VMEM((halves, RING, LANES - PIECE, share), BF16),
+            pltpu.VMEM((halves, RING, LANES - PIECE, share), BF16),
+            pltpu.VMEM((halves, RING, LANES - PIECE, share), F32),
+            pltpu.VMEM((halves, RING, LANES - PIECE, share), BF16),
+            pltpu.VMEM((halves, RING, LANES - PIECE, share), BF16),
             pltpu.VMEM((halves, PIECE, share), BF16),
             pltpu.VMEM((halves, PIECE, share), BF16),
             pltpu.VMEM((halves, LANES, share), F32),

time: 77.4 us -> 76.3 us (0.986)
  Pallas kernels: 76.6 us -> 75.1 us
    pallas_call x1, Pallas kernels: 76.6 us -> 75.1 us  [per_device(): pl.pallas_call(functools.partial(kernel, nc, nt), out_shape=pltpu.VMEM((t...]
where the time goes in v7:
time: 76.3 us; the launch traced here: 75.8 us
  Pallas kernels  75.1 us (98%)
    pallas_call x1, Pallas kernels, per_device(): pl.pallas_call(functools.partial(kernel, nc, nt), out_shape=pltpu.VMEM((t...  75.1 us

profile of v7, /device:TPU:8, one launch (start us, length us, event | category | flops | bytes accessed | tf_op | source)
XLA Modules:
  0.0 75.8 jit_solution(12183641247134820154)
XLA Ops:
  0.0 75.1 %shard_map.109 = bf16[256,512]{1,0:T(8,128)(2,1)S(1)} custom-call(bf16[256,1024]{1,0:T(8,128)(2,1)} %q_hbm.1, bf16[256,1024]{1,0:T(8,128)(2,1)} %k_hbm.1, bf16[256,1024]{1,0:T(8,128)(2,1)} %v_hbm.1, bf16[1024,256]{1,0:T(8,128)(2,1)} %filt_hbm.1, bf16[1024,4096]{1,0:T(8,128)(2,1)} %w_hbm.1, bf16[2,256,256]{2,1,0:T(8,128)(2,1)} %constant.6.clone.fwd_hbm, ...), custom_call_target="tpu_custom_call" | custom-call | tf_op jit(solution)/shard_map/pallas_call | solution.py:680
  75.1 0.7 copy.13

commit v8 on v7

--- a/solution.py
+++ b/solution.py
@@ -468,7 +468,7 @@
     def _(part):
         rows16 = pl.ds(pl.multiple_of(part * PART, PART), PART)
 
-        @pl.loop(0, nc)
+        @pl.loop(0, nc, unroll=True)
         def _(s):
             slot = srecv.at[s, rows16, :]
             pltpu.make_async_copy(slot, slot, sig_recv.at[part, s]).wait()
@@ -624,7 +624,7 @@
             row_copy(c, partner(j, mt, nt)).start()
 
     def normalize(c):
-        @pl.loop(0, nt - 1)
+        @pl.loop(0, nt - 1, unroll=True)
         def _(j):
             p = partner(j, mt, nt)
             slot = srow.at[c, p]

time: 76.3 us -> 75.8 us (level)
  no operation moved by 1% of the time
where the time goes in v8:
time: 75.8 us; the launch traced here: 75.7 us
  Pallas kernels  75 us (99%)
    pallas_call x1, Pallas kernels, per_device(): pl.pallas_call(functools.partial(kernel, nc, nt), out_shape=pltpu.VMEM((t...  75 us

profile of v8, /device:TPU:8, one launch (start us, length us, event | category | flops | bytes accessed | tf_op | source)
XLA Modules:
  0.0 75.7 jit_solution(16833528554425868689)
XLA Ops:
  0.0 75.0 %shard_map.109 = bf16[256,512]{1,0:T(8,128)(2,1)S(1)} custom-call(bf16[256,1024]{1,0:T(8,128)(2,1)} %q_hbm.1, bf16[256,1024]{1,0:T(8,128)(2,1)} %k_hbm.1, bf16[256,1024]{1,0:T(8,128)(2,1)} %v_hbm.1, bf16[1024,256]{1,0:T(8,128)(2,1)} %filt_hbm.1, bf16[1024,4096]{1,0:T(8,128)(2,1)} %w_hbm.1, bf16[2,256,256]{2,1,0:T(8,128)(2,1)} %constant.6.clone.fwd_hbm, ...), custom_call_target="tpu_custom_call" | custom-call | tf_op jit(solution)/shard_map/pallas_call | solution.py:680
  75.0 0.7 copy.13
